TPU v7x, 128 devices: a whole 4x4x4 slice. The times are simulated.
128 devices in a mesh: dom: 32 (over y, z, core), tm: 4 (over x).
Axes of the slice: x: 4, y: 4, z: 4, core: 2. Of those that a mesh axis runs over, the one named last changes fastest.
Arguments:
- panel_signal: bfloat16 [8, 32768], P('tm', 'dom'), may hold values from -6 to 6
- panel_box: int32 [32768], P('dom'), may hold values from 0 to 15
- radiation: bfloat16 [32768, 1024], P('dom'), may hold values from -0.75 to 0.75
- reception: bfloat16 [32768, 1024], P('dom'), may hold values from -0.1875 to 0.1875
- translation: bfloat16 [64, 8, 1024], P(None, None, 'dom'), may hold values from -1 to 1
- list_source: int32 [512, 8], replicated, may hold values from 0 to 511
- list_class: int32 [512, 8], replicated, may hold values from 0 to 63
- list_count: int32 [512], replicated, may hold values from 1 to 8, as said below
Outputs:
- panel_field: bfloat16 [8, 32768], P('tm', 'dom')
Inputs may be any that keep to these rules, and one draw needn't show every extreme that they name: `panel_box`: indices a panel's box among the 16 boxes of its own index of dom. Box a uses the first list_count[a] entries of its lists; the rest are padding.
All inputs are finite; a program needn't handle non-finite values.
Results may differ from a plain program's by a relative error of at most 0.0057.
Values may be sent and summed in bfloat16 or wider, within the bound.
No kernel may reach another device: no remote copies, remote signals or barrier semaphores. Data moves between devices by JAX's collectives and lax.ppermute only.
A program may use at most 64 MiB of HBM per device.

v0:
```python
import math

import jax
import jax.numpy as jnp
from jax import lax
from jax.sharding import PartitionSpec as P

BOX_DEV = 16
J = 8


def lag_sum(kern_rows, gathered, out_steps, offset):
    entries = kern_rows.shape[0]
    lags_all = kern_rows.shape[1]
    width = kern_rows.shape[2]
    results = []
    for step_out in range(out_steps):
        total = jnp.zeros((entries, width), jnp.float32)
        for step_in in range(gathered.shape[1]):
            delay = offset + step_out - step_in
            picked = lax.dynamic_index_in_dim(
                kern_rows, jnp.clip(delay, 0, lags_all - 1), 1, keepdims=False
            )
            weight = jnp.where(delay >= 0, picked.astype(jnp.float32), 0.0)
            total = total + weight * gathered[:, step_in].astype(jnp.float32)
        results.append(total)
    return jnp.stack(results, axis=1)


def body(
    panel_signal, panel_box, radiation, reception, translation, list_source, list_class, list_count
):
    rows_own = panel_signal.shape[0]
    dirs_own = translation.shape[2]
    boxes_all = list_source.shape[0]
    classes_all = translation.shape[0]
    lags_all = translation.shape[1]
    box_onehot = (panel_box[None, :] == jnp.arange(BOX_DEV, dtype=jnp.int32)[:, None]).astype(
        jnp.bfloat16
    )
    used_rows = (jnp.arange(J, dtype=jnp.int32)[None, :] < list_count[:, None]).astype(jnp.bfloat16)
    block_size = math.gcd(boxes_all, 256)

    def translate_all(table, rays, out_steps, offset):
        width = table.shape[2]
        count_in = rays.shape[1]
        flat_table = table.reshape(classes_all, lags_all * width)
        flat_rays = rays.reshape(boxes_all, count_in * width)

        def one_block(index):
            sources = lax.dynamic_slice_in_dim(
                list_source, index * block_size, block_size, 0
            ).reshape(block_size * J)
            classes = lax.dynamic_slice_in_dim(
                list_class, index * block_size, block_size, 0
            ).reshape(block_size * J)
            keep_rows = lax.dynamic_slice_in_dim(
                used_rows, index * block_size, block_size, 0
            ).reshape(block_size * J, 1)
            kern_rows = (jnp.take(flat_table, classes, axis=0) * keep_rows).reshape(
                block_size * J, lags_all, width
            )
            gathered = jnp.take(flat_rays, sources, axis=0).reshape(block_size * J, count_in, width)
            summed = lag_sum(kern_rows, gathered, out_steps, offset)
            return jnp.sum(summed.reshape(block_size, J, out_steps, width), axis=1)

        blocks = lax.map(one_block, jnp.arange(boxes_all // block_size, dtype=jnp.int32))
        return blocks.reshape(boxes_all, out_steps, width)

    masked = panel_signal[:, None, :] * box_onehot[None]
    outgoing = jnp.einsum(
        "rbp,pk->brk", masked, radiation, preferred_element_type=jnp.float32
    ).astype(jnp.bfloat16)
    spread = lax.all_to_all(outgoing, "dom", split_axis=2, concat_axis=0, tiled=True)
    first = lax.axis_index("tm") * rows_own
    empty = jnp.zeros((boxes_all, rows_own, dirs_own), jnp.float32)
    piece = lax.all_gather(spread, "tm", axis=1, tiled=True)

    def active():
        return empty + translate_all(translation, piece, rows_own, first)

    def passive():
        return empty

    incoming = lax.cond(jnp.int32(0) <= first + rows_own - 1, active, passive)
    rays = lax.all_to_all(
        incoming.astype(jnp.bfloat16), "dom", split_axis=0, concat_axis=2, tiled=True
    )
    partial_value = jnp.einsum("brk,pk->brp", rays, reception, preferred_element_type=jnp.float32)
    field = jnp.sum(partial_value * box_onehot.astype(jnp.float32)[:, None, :], axis=0)
    return field.astype(jnp.bfloat16)


def solution(mesh):
    placed = (
        P("tm", "dom"),
        P("dom"),
        P("dom", None),
        P("dom", None),
        P(None, None, "dom"),
        P(),
        P(),
        P(),
    )
    return jax.shard_map(
        body, mesh=mesh, in_specs=placed, out_specs=P("tm", "dom"), check_vma=False
    )
```

profile of v0, /device:TPU:1, one launch (start us, length us, event | category | flops | bytes accessed | tf_op | source)
XLA Modules:
  0.0 120.6 jit_solution(1148992398385621350)
XLA Ops:
  1.6 1.1 fusion.27
  3.2 1.2 reshape.218
  4.4 9.6 %all-to-all-start = ((bf16[32,2,512]{2,1,0:T(2,128)(2,1)}), bf16[32,2,512]{2,1,0:T(2,128)(2,1)S(1)}, u32[]{:S(2)}, u32[]{:S(2)}) async-start(bf16[32,2,512]{2,1,0:T(2,128)(2,1)} %reshape.218), calls=%async_computation | async-start | bytes 131072 | tf_op jit(solution)/shard_map/all_to_all | solution.py:74
  14.8 6.6 %all-to-all-done = bf16[32,2,512]{2,1,0:T(2,128)(2,1)S(1)} async-done(((bf16[32,2,512]{2,1,0:T(2,128)(2,1)}), bf16[32,2,512]{2,1,0:T(2,128)(2,1)S(1)}, u32[]{:S(2)}, u32[]{:S(2)}) %all-to-all-start) | async-done | bytes 65568 | tf_op jit(solution)/shard_map/all_to_all | solution.py:74
  22.3 10.2 %all_gather.3 = bf16[512,8,32]{0,2,1:T(8,128)(2,1)S(1)} all-gather(bf16[512,2,32]{0,2,1:T(8,128)(2,1)S(1)} %copy.59), channel_id=1, replica_groups=mesh['dom'=32,'tm'=4] {'tm'}, dimensions={1}, use_global_device_ids=true | all-gather | bytes 327680 | tf_op jit(solution)/shard_map/all_gather | solution.py:77
  32.5 70.1 %conditional.1 = (bf16[512,2,32]{2,1,0:T(2,128)(2,1)}) conditional(s32[]{:T(128)} %convert_element_type.232, () %tuple.28, (bf16[64,8,32]{0,2,1:T(8,128)(2,1)S(1)}, bf16[512,8,32]{0,2,1:T(8,128)(2,1)S(1)}, s32[]{:T(128)}, s32[512,8]{0,1:T(8,128)S(1)}, bf16[512,8]{1,0:T(8,128)(2,1)}, /*index=5*/s32[512,8]{0,1:T(8,128)}) %tuple.57), branch_computations={%region_0.0_spmd, %region_1.5_spmd} | conditional | flops 6971433 | bytes 19919924 | solution.py:85
  32.8 69.8 %while.13 = (s32[]{:T(128)}, bf16[2,256,2,32]{3,2,1,0:T(2,128)(2,1)}, pred[]{:T(512)}, s32[2]{0:T(128)S(1)}, s32[512,8]{0,1:T(8,128)S(1)}, /*index=5*/bf16[64,25...) while((s32[]{:T(128)}, ...), condition=%wide.region_4.4_spmd, body=%wide.region_2.3_spmd.sunk | while | flops 6971398 | bytes 19329444 | solution.py:67
  36.4 7.5 %gather_fusion.1 = bf16[2048,256]{1,0:T(8,128)(2,1)S(1)} fusion(bf16[512,256]{1,0:T(8,128)(2,1)S(1)} %get-tuple-element.1064, s32[2048]{0:T(1024)S(1)} %broadcast_clamp_fusion.5), kind=kCustom, calls=%fused_computation.1.clone.1 | custom fusion | bytes 2105344 | tf_op jit(solution)/shard_map/cond/branch_1_fun/while/body/eval_jaxpr/jit(_take)/gather | solution.py:63
  43.9 1.4 %copy.81 = bf16[2048,256]{0,1:T(8,128)(2,1)} copy(bf16[2048,256]{1,0:T(8,128)(2,1)S(1)} %gather_fusion.1) | data formatting | bytes 2097152 | tf_op jit(solution)/shard_map/cond/branch_1_fun/while/body/eval_jaxpr/jit(_take)/gather | solution.py:63
  45.4 1.3 %broadcast_select_fusion.2 = bf16[2048,8,32]{0,2,1:T(8,128)(2,1)S(1)} fusion(bf16[2048,8,32]{0,2,1:T(8,128)(2,1)} %bitcast.60, pred[2048]{0:T(1024)(128)(4,1)S(1)} %compare_and_fusion.5), kind=kLoop, calls=%fused_computation.4.clone.1 | loop fusion | flops 524288 | bytes 2099200 | tf_op jit(solution)/shard_map/cond/branch_1_fun/while/body/eval_jaxpr/jit(_take)/select_n | solution.py:63
  46.7 9.0 %gather_fusion = bf16[2048,256]{1,0:T(8,128)(2,1)} fusion(bf16[64,256]{1,0:T(8,128)(2,1)S(1)} %get-tuple-element.1060, s32[2048]{0:T(1024)S(1)} %broadcast_clamp_fusion.4), kind=kCustom, calls=%fused_computation.clone.1 | custom fusion | bytes 2105344 | tf_op jit(solution)/shard_map/cond/branch_1_fun/while/body/eval_jaxpr/jit(_take)/gather | solution.py:60
  55.7 2.3 %copy.79 = bf16[2048,256]{0,1:T(8,128)(2,1)} copy(bf16[2048,256]{1,0:T(8,128)(2,1)} %gather_fusion) | data formatting | bytes 2097152 | tf_op jit(solution)/shard_map/cond/branch_1_fun/while/body/eval_jaxpr/jit(_take)/gather | solution.py:60
  58.0 1.3 %select_multiply_fusion.2 = bf16[2048,8,32]{0,2,1:T(8,128)(2,1)S(1)} fusion(bf16[2048,8,32]{0,2,1:T(8,128)(2,1)} %bitcast.58, pred[2048]{0:T(1024)(128)(4,1)S(1)} %compare_and_fusion.4, bf16[2048]{0:T(1024)(128)(2,1)S(1)} %mul.312), kind=kLoop, calls=%fused_computation.3.clone.1 | loop fusion | flops 1048576 | bytes 2103296 | tf_op jit(solution)/shard_map/cond/branch_1_fun/while/body/eval_jaxpr/mul | solution.py:60
  59.3 1.1 fusion.40
  60.4 1.1 fusion.39
  61.4 1.3 %copy.82 = f32[2048,1,32]{2,0,1:T(8,128)S(1)} copy(f32[2048,1,32]{0,2,1:T(8,128)} %fusion.39) | data formatting | bytes 524288 | tf_op jit(solution)/shard_map/cond/branch_1_fun/while/body/eval_jaxpr/add | solution.py:25
  62.7 2.3 %copy.83 = f32[2048,1,32]{2,0,1:T(8,128)} copy(f32[2048,1,32]{0,2,1:T(8,128)} %fusion.40) | data formatting | bytes 524288 | tf_op jit(solution)/shard_map/cond/branch_1_fun/while/body/eval_jaxpr/add | solution.py:25
  65.0 1.9 %maximum_reduce_fusion.2 = bf16[256,2,32]{2,0,1:T(8,128)(2,1)S(1)} fusion(f32[256,8,1,32]{3,1,0,2:T(8,128)S(1)} %bitcast.59, f32[256,8,1,32]{3,1,0,2:T(8,128)} %bitcast.61), kind=kLoop, calls=%fused_computation.2.clone.1 | loop fusion | flops 245760 | bytes 557056 | tf_op jit(solution)/shard_map/cond/branch_1_fun/while/body/eval_jaxpr/reduce_sum | solution.py:65
  71.3 7.5 %gather_fusion.1 = bf16[2048,256]{1,0:T(8,128)(2,1)S(1)} fusion(bf16[512,256]{1,0:T(8,128)(2,1)S(1)} %get-tuple-element.1064, s32[2048]{0:T(1024)S(1)} %broadcast_clamp_fusion.5), kind=kCustom, calls=%fused_computation.1.clone.1 | custom fusion | bytes 2105344 | tf_op jit(solution)/shard_map/cond/branch_1_fun/while/body/eval_jaxpr/jit(_take)/gather | solution.py:63
  78.8 1.4 %copy.81 = bf16[2048,256]{0,1:T(8,128)(2,1)} copy(bf16[2048,256]{1,0:T(8,128)(2,1)S(1)} %gather_fusion.1) | data formatting | bytes 2097152 | tf_op jit(solution)/shard_map/cond/branch_1_fun/while/body/eval_jaxpr/jit(_take)/gather | solution.py:63
  80.3 1.3 %broadcast_select_fusion.2 = bf16[2048,8,32]{0,2,1:T(8,128)(2,1)S(1)} fusion(bf16[2048,8,32]{0,2,1:T(8,128)(2,1)} %bitcast.60, pred[2048]{0:T(1024)(128)(4,1)S(1)} %compare_and_fusion.5), kind=kLoop, calls=%fused_computation.4.clone.1 | loop fusion | flops 524288 | bytes 2099200 | tf_op jit(solution)/shard_map/cond/branch_1_fun/while/body/eval_jaxpr/jit(_take)/select_n | solution.py:63
  81.6 9.0 %gather_fusion = bf16[2048,256]{1,0:T(8,128)(2,1)} fusion(bf16[64,256]{1,0:T(8,128)(2,1)S(1)} %get-tuple-element.1060, s32[2048]{0:T(1024)S(1)} %broadcast_clamp_fusion.4), kind=kCustom, calls=%fused_computation.clone.1 | custom fusion | bytes 2105344 | tf_op jit(solution)/shard_map/cond/branch_1_fun/while/body/eval_jaxpr/jit(_take)/gather | solution.py:60
  90.6 2.3 %copy.79 = bf16[2048,256]{0,1:T(8,128)(2,1)} copy(bf16[2048,256]{1,0:T(8,128)(2,1)} %gather_fusion) | data formatting | bytes 2097152 | tf_op jit(solution)/shard_map/cond/branch_1_fun/while/body/eval_jaxpr/jit(_take)/gather | solution.py:60
  92.9 1.3 %select_multiply_fusion.2 = bf16[2048,8,32]{0,2,1:T(8,128)(2,1)S(1)} fusion(bf16[2048,8,32]{0,2,1:T(8,128)(2,1)} %bitcast.58, pred[2048]{0:T(1024)(128)(4,1)S(1)} %compare_and_fusion.4, bf16[2048]{0:T(1024)(128)(2,1)S(1)} %mul.312), kind=kLoop, calls=%fused_computation.3.clone.1 | loop fusion | flops 1048576 | bytes 2103296 | tf_op jit(solution)/shard_map/cond/branch_1_fun/while/body/eval_jaxpr/mul | solution.py:60
  94.2 1.1 fusion.40
  95.3 1.1 fusion.39
  96.3 1.3 %copy.82 = f32[2048,1,32]{2,0,1:T(8,128)S(1)} copy(f32[2048,1,32]{0,2,1:T(8,128)} %fusion.39) | data formatting | bytes 524288 | tf_op jit(solution)/shard_map/cond/branch_1_fun/while/body/eval_jaxpr/add | solution.py:25
  97.6 2.3 %copy.83 = f32[2048,1,32]{2,0,1:T(8,128)} copy(f32[2048,1,32]{0,2,1:T(8,128)} %fusion.40) | data formatting | bytes 524288 | tf_op jit(solution)/shard_map/cond/branch_1_fun/while/body/eval_jaxpr/add | solution.py:25
  99.9 1.9 %maximum_reduce_fusion.2 = bf16[256,2,32]{2,0,1:T(8,128)(2,1)S(1)} fusion(f32[256,8,1,32]{3,1,0,2:T(8,128)S(1)} %bitcast.59, f32[256,8,1,32]{3,1,0,2:T(8,128)} %bitcast.61), kind=kLoop, calls=%fused_computation.2.clone.1 | loop fusion | flops 245760 | bytes 557056 | tf_op jit(solution)/shard_map/cond/branch_1_fun/while/body/eval_jaxpr/reduce_sum | solution.py:65
  102.6 1.2 reshape.220
  103.8 13.3 %all_to_all.36 = bf16[32,2,512]{2,1,0:T(2,128)(2,1)S(1)} all-to-all(bf16[32,2,512]{2,1,0:T(2,128)(2,1)S(1)} %reshape.220), channel_id=1, replica_groups=mesh['dom'=32,'tm'=4] {'dom'}, dimensions={0} | all-to-all | bytes 131072 | tf_op jit(solution)/shard_map/all_to_all | solution.py:86
  117.6 2.9 %fusion.24 = bf16[2,1024]{1,0:T(2,128)(2,1)} fusion(bf16[16,2,1024]{2,0,1:T(8,128)(2,1)S(1)} %all_to_all.33, bf16[1024,1024]{1,0:T(8,128)(2,1)} %param.15, f32[16,1024]{1,0:T(8,128)S(1)} %get-tuple-element.832), kind=kOutput, calls=%fused_computation.60 | convolution fusion | flops 67172352 | bytes 2232320 | tf_op jit(solution)/shard_map/brk,pk->brp/dot_general | solution.py:89
  (55 shorter events, 12.1 us)
Async XLA Ops:
  0.0 1.6 %copy-start = (bf16[1024,1024]{1,0:T(8,128)(2,1)S(1)}, bf16[1024,1024]{1,0:T(8,128)(2,1)}, u32[]{:S(2)}) copy-start(bf16[1024,1024]{1,0:T(8,128)(2,1)} %param.14) | copy-start | bytes 6291460
  0.0 14.0 %copy-start.3 = (s32[512]{0:T(512)S(1)}, s32[512]{0:T(512)}, u32[]{:S(2)}) copy-start(s32[512]{0:T(512)} %param.19) | copy-start | bytes 6148
  2.8 29.8 %copy-start.1 = (s32[512,8]{0,1:T(8,128)S(1)}, s32[512,8]{0,1:T(8,128)}, u32[]{:S(2)}) copy-start(s32[512,8]{0,1:T(8,128)} %param.18) | copy-start | bytes 49156
  2.8 29.7 %copy-start.2 = (bf16[64,8,32]{0,2,1:T(8,128)(2,1)S(1)}, bf16[64,8,32]{0,2,1:T(8,128)(2,1)}, u32[]{:S(2)}) copy-start(bf16[64,8,32]{0,2,1:T(8,128)(2,1)} %param.16) | copy-start | bytes 98308
  4.4 17.0 %all-to-all-start = ((bf16[32,2,512]{2,1,0:T(2,128)(2,1)}), bf16[32,2,512]{2,1,0:T(2,128)(2,1)S(1)}, u32[]{:S(2)}, u32[]{:S(2)}) async-start(bf16[32,2,512]{2,1,0:T(2,128)(2,1)} %reshape.218), calls=%async_computation | async-start | bytes 131072 | tf_op jit(solution)/shard_map/all_to_all | solution.py:74
where the time goes:
time: 121 us
  local copies, waits for them, and re-layouts  60.3 us (50%)
  blocking collectives  23.5 us (19%)
  other arithmetic  15.1 us (12%)
  starting transfers between devices  9.6 us (8%)
  waiting for transfers between devices  6.57 us (5%)
  matrix products  4.08 us (3%)
  loops' own time  1.39 us (1%)
    gather x4, local copies, waits for them, and re-layouts, one_block(): jnp.take(flat_table, classes, axis=0) * keep_rows  22.6 us
    gather x4, local copies, waits for them, and re-layouts, one_block(): jnp.take(flat_rays, sources, axis=0)  17.8 us
    all_to_all x1, blocking collectives, body(): lax.all_to_all(incoming.astype(jnp.bfloat16), 'dom', split_axis=0, concat...  13.3 us
    all_gather x1, blocking collectives, body(): piece = lax.all_gather(spread, 'tm', axis=1, tiled=True)  10.2 us
    all_to_all x1, starting transfers between devices, body(): lax.all_to_all(outgoing, 'dom', split_axis=2, concat_axis=0, tiled=True)  9.6 us
    add x4, local copies, waits for them, and re-layouts, lag_sum(): total = total + weight * gathered[:, step_in].astype(jnp.float32)  7.09 us
    all_to_all x1, waiting for transfers between devices, body(): lax.all_to_all(outgoing, 'dom', split_axis=2, concat_axis=0, tiled=True)  6.57 us
    add x4, other arithmetic, lag_sum(): total = total + weight * gathered[:, step_in].astype(jnp.float32)  4.25 us
  transfers between devices with their start and end apart: 1, of which 1 were waited for; matrix products, arithmetic and copies ran while one was open for 1% of the time, Pallas kernels for 0%

commit v1 on v0

v1 whole, which is shorter than its diff:
```python
import jax
import jax.numpy as jnp
from jax import lax
from jax.experimental import pallas as pl
from jax.experimental.pallas import tpu as pltpu
from jax.sharding import PartitionSpec as P

BOX_DEV = 16
J = 8
N_DOM = 32
N_TM = 4
DIRS = 32
LAGS = 8
CLASSES = 64
BOXES = 512
PAN_DEV = 1024
K = 1024
GROUPS = K // 128
CHUNK = 128
N_CHUNK = BOXES // CHUNK
VMEM = pl.BlockSpec(memory_space=pltpu.VMEM)


def owner_rows(box_ref, half):
    row = lax.broadcasted_iota(jnp.int32, (8, PAN_DEV), 0) + 8 * half
    return box_ref[...] == row


def lane_group(shape):
    return lax.broadcasted_iota(jnp.int32, shape, len(shape) - 1) // DIRS


def aggregate_kernel(signal_ref, box_ref, radiation_ref, out_ref):
    signal = signal_ref[...].astype(jnp.float32)
    parts = []
    for half in range(2):
        mine = owner_rows(box_ref, half)
        for step in range(2):
            parts.append(jnp.where(mine, signal[step : step + 1, :], 0.0))
    masked = jnp.concatenate(parts, axis=0).astype(jnp.bfloat16)
    rays = jnp.dot(masked, radiation_ref[...], preferred_element_type=jnp.float32)
    group = lane_group((8, 128))
    for column in range(GROUPS):
        block = [rays[q * 8 : q * 8 + 8, column * 128 : column * 128 + 128] for q in range(4)]
        for g in range(4):
            tile = None
            for q in range(4):
                turn = ((q - g) % 4) * DIRS
                moved = block[q] if turn == 0 else pltpu.roll(block[q], turn, 1)
                tile = moved if tile is None else jnp.where(group == q, moved, tile)
            tile = tile.astype(jnp.bfloat16)
            for plane in range(N_TM):
                out_ref[(column * 4 + g) * N_TM + plane] = tile


def tables_kernel(source_ref, class_ref, count_ref, table_ref, pick_ref, weight_ref, rhs_ref):
    first = lax.axis_index("tm") * 2
    for step_out in range(2):
        for step_in in range(LAGS):
            lag = first + step_out - step_in
            start = pl.multiple_of(jnp.maximum(lag, 0) * DIRS, DIRS)
            rows = table_ref[pl.ds(start, DIRS), :]
            rows = jnp.where(lag >= 0, rows, jnp.zeros_like(rows))
            rhs_ref[pl.ds((step_out * LAGS + step_in) * DIRS, DIRS), :] = rows
    sources = source_ref[...]
    used = lax.broadcasted_iota(jnp.int32, (J, BOXES), 0) < count_ref[...]
    classes = jnp.where(used, class_ref[...], -1)
    sources = jnp.transpose(sources)
    classes = jnp.transpose(classes)
    lane_s = lax.broadcasted_iota(jnp.int32, (CHUNK, BOXES), 1)
    lane_c = lax.broadcasted_iota(jnp.int32, (CHUNK, CLASSES), 1)
    rhs = rhs_ref[...]
    for chunk in range(N_CHUNK):
        for j in range(J):
            rows = slice(chunk * CHUNK, chunk * CHUNK + CHUNK)
            at = pl.ds((chunk * J + j) * CHUNK, CHUNK)
            src = sources[rows, j : j + 1]
            cls = classes[rows, j : j + 1]
            pick_ref[at, :] = (src == lane_s).astype(jnp.float32).astype(jnp.bfloat16)
            hot = (cls == lane_c).astype(jnp.float32).astype(jnp.bfloat16)
            weight_ref[at, :] = lax.dot_general(
                hot, rhs, (((1,), (1,)), ((), ())), preferred_element_type=jnp.float32
            )


def translate_kernel(rays_ref, pick_ref, weight_ref, out_ref, near_ref, got_ref, sum_ref):
    low = lax.broadcasted_iota(jnp.int32, (N_DOM, 8, 128), 2) < 64
    for pair in range(2):
        left = rays_ref[:, 2 * pair].astype(jnp.float32)
        right = rays_ref[:, 2 * pair + 1].astype(jnp.float32)
        upper = jnp.where(low, left, pltpu.roll(right, 64, 2))
        lower = jnp.where(low, pltpu.roll(left, 64, 2), right)
        both = jnp.concatenate([upper[:, None], lower[:, None]], axis=1)
        near_ref[:, pair * 128 : pair * 128 + 128] = both.reshape(BOXES, 128).astype(jnp.bfloat16)
    rows_chunk = J * CHUNK
    for chunk in range(N_CHUNK):
        base = chunk * rows_chunk
        got_ref[...] = jnp.dot(
            pick_ref[base : base + rows_chunk, :],
            near_ref[...],
            preferred_element_type=jnp.float32,
        )
        for piece in range(CHUNK // 16):
            total = [jnp.zeros((16, 128), jnp.float32) for _ in range(2)]
            for j in range(J):
                at = j * CHUNK + piece * 16
                for side in range(2):
                    got = got_ref[at : at + 16, side * 128 : side * 128 + 128]
                    for step in range(2):
                        lanes = slice(step * 256 + side * 128, step * 256 + side * 128 + 128)
                        total[step] = total[step] + weight_ref[base + at : base + at + 16, lanes] * got
            for step in range(2):
                at = chunk * CHUNK + piece * 16
                sum_ref[at : at + 16, step * 128 : step * 128 + 128] = total[step]
    even = lane_group((N_DOM, 8, 128)) % 2 == 0
    merged = []
    for half in range(2):
        one = sum_ref[:, 0:128].reshape(N_DOM, 2, 8, 128)[:, half]
        two = sum_ref[:, 128:256].reshape(N_DOM, 2, 8, 128)[:, half]
        merged.append(
            jnp.where(even, one, two)
            + jnp.where(even, pltpu.roll(one, 96, 2), pltpu.roll(two, 32, 2))
        )
    final = jnp.where(low, merged[0], merged[1]) + pltpu.roll(
        jnp.where(low, merged[1], merged[0]), 64, 2
    )
    out_ref[...] = final.astype(jnp.bfloat16)


def receive_kernel(rays_ref, box_ref, reception_ref, out_ref):
    rays = rays_ref[...].astype(jnp.float32)
    turned = [rays] + [pltpu.roll(rays, DIRS * turn, 2) for turn in range(1, 4)]
    group = lane_group((8, 128))
    rows = []
    for q in range(4):
        columns = []
        for column in range(GROUPS):
            tile = None
            for g in range(4):
                moved = turned[(g - q) % 4][column * 4 + g]
                tile = moved if tile is None else jnp.where(group == g, moved, tile)
            columns.append(tile)
        rows.append(jnp.concatenate(columns, axis=1))
    incoming = jnp.concatenate(rows, axis=0).astype(jnp.bfloat16)
    field = lax.dot_general(
        incoming, reception_ref[...], (((1,), (1,)), ((), ())), preferred_element_type=jnp.float32
    )
    steps = []
    for step in range(2):
        total = jnp.zeros((1, PAN_DEV), jnp.float32)
        for half in range(2):
            q = half * 2 + step
            kept = jnp.where(owner_rows(box_ref, half), field[q * 8 : q * 8 + 8, :], 0.0)
            total = total + jnp.sum(kept, axis=0, keepdims=True)
        steps.append(total)
    out_ref[...] = jnp.concatenate(steps, axis=0).astype(jnp.bfloat16)


def params(mib):
    return pltpu.CompilerParams(vmem_limit_bytes=mib << 20)


def body(
    panel_signal, panel_box, radiation, reception, translation, list_source, list_class, list_count
):
    boxes_row = panel_box.reshape(1, PAN_DEV)
    blocks = pl.pallas_call(
        aggregate_kernel,
        out_shape=jax.ShapeDtypeStruct((N_DOM * N_TM, 8, 128), jnp.bfloat16),
        in_specs=[VMEM] * 3,
        out_specs=VMEM,
        compiler_params=params(16),
        name="aggregate",
    )(panel_signal, boxes_row, radiation)
    spread = lax.all_to_all(blocks, ("dom", "tm"), split_axis=0, concat_axis=0, tiled=True)

    pick, weight = pl.pallas_call(
        tables_kernel,
        out_shape=(
            jax.ShapeDtypeStruct((BOXES * J, BOXES), jnp.bfloat16),
            jax.ShapeDtypeStruct((BOXES * J, 2 * LAGS * DIRS), jnp.float32),
        ),
        in_specs=[VMEM] * 4,
        out_specs=(VMEM, VMEM),
        scratch_shapes=[pltpu.VMEM((2 * LAGS * DIRS, CLASSES), jnp.bfloat16)],
        compiler_params=params(32),
        cost_estimate=pl.CostEstimate(
            flops=2 * 4096 * 64 * 512, bytes_accessed=12 << 20, transcendentals=0
        ),
        name="tables",
    )(
        list_source.T,
        list_class.T,
        list_count.reshape(1, BOXES),
        jnp.transpose(translation, (1, 2, 0)).reshape(LAGS * DIRS, CLASSES),
    )

    incoming = pl.pallas_call(
        translate_kernel,
        out_shape=jax.ShapeDtypeStruct((N_DOM, 8, 128), jnp.bfloat16),
        in_specs=[VMEM] * 3,
        out_specs=VMEM,
        scratch_shapes=[
            pltpu.VMEM((BOXES, 256), jnp.bfloat16),
            pltpu.VMEM((J * CHUNK, 256), jnp.float32),
            pltpu.VMEM((BOXES, 256), jnp.float32),
        ],
        compiler_params=params(32),
        name="translate",
    )(spread.reshape(N_DOM, N_TM, 8, 128), pick, weight)

    rays = lax.all_to_all(incoming, "dom", split_axis=0, concat_axis=0, tiled=True)
    return pl.pallas_call(
        receive_kernel,
        out_shape=jax.ShapeDtypeStruct((2, PAN_DEV), jnp.bfloat16),
        in_specs=[VMEM] * 3,
        out_specs=VMEM,
        compiler_params=params(16),
        name="receive",
    )(rays, boxes_row, reception)


def solution(mesh):
    placed = (
        P("tm", "dom"),
        P("dom"),
        P("dom", None),
        P("dom", None),
        P(None, None, "dom"),
        P(),
        P(),
        P(),
    )
    return jax.shard_map(
        body, mesh=mesh, in_specs=placed, out_specs=P("tm", "dom"), check_vma=False
    )
```

time: 121 us -> 49.7 us (0.41)
  local copies, waits for them, and re-layouts: 60.3 us -> 16.7 us
  other arithmetic: 15.1 us -> 0 us
  blocking collectives: 23.5 us -> 13.5 us
  Pallas kernels: 0 us -> 5.89 us
  waiting for transfers between devices: 6.57 us -> 1.5 us
  matrix products: 4.08 us -> 0 us
  starting transfers between devices: 9.6 us -> 11.5 us
  loops' own time: 1.39 us -> 0 us
    gather x8 -> x0, local copies, waits for them, and re-layouts: 40.4 us -> none  [the longest x4 22.6 us: one_block(): jnp.take(flat_table, classes, axis=0) * keep_rows]
    unnamed x12 -> x26, local copies, waits for them, and re-layouts: 3.73 us -> 16.7 us
    all_gather x1 -> x0, blocking collectives: 10.2 us -> none  [body(): piece = lax.all_gather(spread, 'tm', axis=1, tiled=True)]
    add x4 -> x0, local copies, waits for them, and re-layouts: 7.09 us -> none  [lag_sum(): total = total + weight * gathered[:, step_in].astype(jnp.float32)]
    pallas_call x0 -> x4, Pallas kernels: none -> 5.89 us  [the longest x1 1.68 us: body(): pl.pallas_call(tables_kernel, out_shape=(jax.ShapeDtypeStruct((BOXES * J,...]
    all_to_all x1, waiting for transfers between devices: 6.57 us -> 1.5 us  [body(): lax.all_to_all(blocks, ('dom', 'tm'), split_axis=0, concat_axis=0, tiled=...]
    dynamic_slice x10 -> x0, local copies, waits for them, and re-layouts: 4.73 us -> none  [the longest x2 1.69 us: one_block(): lax.dynamic_slice_in_dim(used_rows, index * block_size, block_size, 0)]
    add x4 -> x0, other arithmetic: 4.25 us -> none  [lag_sum(): total = total + weight * gathered[:, step_in].astype(jnp.float32)]
  transfers between devices with their start and end apart: 1 -> 1, of which waited for: 1 -> 1; matrix products, arithmetic and copies ran while one was open for 1% -> 0% of each run, Pallas kernels for 0% -> 3%
where the time goes in v1:
time: 49.7 us; the launch traced here: 49.1 us
  local copies, waits for them, and re-layouts  16.7 us (34%)
  blocking collectives  13.5 us (27%)
  starting transfers between devices  11.5 us (23%)
  Pallas kernels  5.89 us (12%)
  waiting for transfers between devices  1.5 us (3%)
    unnamed x26, local copies, waits for them, and re-layouts  16.7 us
    all_to_all x1, blocking collectives, body(): lax.all_to_all(incoming, 'dom', split_axis=0, concat_axis=0, tiled=True)  13.5 us
    all_to_all x1, starting transfers between devices, body(): lax.all_to_all(blocks, ('dom', 'tm'), split_axis=0, concat_axis=0, tiled=...  11.5 us
    pallas_call x1, Pallas kernels, body(): pl.pallas_call(tables_kernel, out_shape=(jax.ShapeDtypeStruct((BOXES * J,...  1.68 us
    pallas_call x1, Pallas kernels, body(): pl.pallas_call(translate_kernel, out_shape=jax.ShapeDtypeStruct((N_DOM, 8...  1.58 us
    all_to_all x1, waiting for transfers between devices, body(): lax.all_to_all(blocks, ('dom', 'tm'), split_axis=0, concat_axis=0, tiled=...  1.5 us
    pallas_call x1, Pallas kernels, body(): pl.pallas_call(receive_kernel, out_shape=jax.ShapeDtypeStruct((2, PAN_DEV...  1.36 us
    pallas_call x1, Pallas kernels, body(): pl.pallas_call(aggregate_kernel, out_shape=jax.ShapeDtypeStruct((N_DOM *...  1.27 us
  transfers between devices with their start and end apart: 1, of which 1 were waited for; matrix products, arithmetic and copies ran while one was open for 0% of the time, Pallas kernels for 3%

profile of v1, /device:TPU:1, one launch (start us, length us, event | category | flops | bytes accessed | tf_op | source)
XLA Modules:
  0.0 49.1 jit_solution(1150870836798006661)
XLA Ops:
  0.0 0.0 copy-start.4
  0.0 1.6 %copy-done.4 = bf16[1024,1024]{1,0:T(8,128)(2,1)S(1)} copy-done((bf16[1024,1024]{1,0:T(8,128)(2,1)S(1)}, bf16[1024,1024]{1,0:T(8,128)(2,1)}, u32[]{:S(2)}) %copy-start.4) | copy-done | bytes 2097176
  1.6 0.0 copy-start.6
  1.6 0.7 %copy-done.6 = s32[1024]{0:T(1024)S(1)} copy-done((s32[1024]{0:T(1024)S(1)}, s32[1024]{0:T(1024)}, u32[]{:S(2)}) %copy-start.6) | copy-done | bytes 4120
  2.3 0.0 copy-start.8
  2.3 0.7 %copy-done.8 = bf16[2,1024]{1,0:T(2,128)(2,1)S(1)} copy-done((bf16[2,1024]{1,0:T(2,128)(2,1)S(1)}, bf16[2,1024]{1,0:T(2,128)(2,1)}, u32[]{:S(2)}) %copy-start.8) | copy-done | bytes 4120
  3.0 1.3 %aggregate.1 = bf16[128,8,128]{2,1,0:T(8,128)(2,1)} custom-call(bf16[2,1024]{1,0:T(2,128)(2,1)S(1)} %copy-done.8, s32[1,1024]{1,0:T(1,128)S(1)} %bitcast.9, bf16[1024,1024]{1,0:T(8,128)(2,1)S(1)} %copy-done.4), custom_call_target="tpu_custom_call" | custom-call | tf_op jit(solution)/shard_map/aggregate/pallas_call | solution.py:167
  4.2 11.5 %all-to-all-start = ((bf16[128,8,128]{2,1,0:T(8,128)(2,1)}), bf16[128,8,128]{2,1,0:T(8,128)(2,1)S(1)}, u32[]{:S(2)}, u32[]{:S(2)}) async-start(bf16[128,8,128]{2,1,0:T(8,128)(2,1)} %aggregate.1), calls=%async_computation | async-start | bytes 524288 | tf_op jit(solution)/shard_map/all_to_all | solution.py:175
  15.7 0.0 copy-start.9
  15.8 0.8 %copy-done.9 = bf16[64,8,32]{0,2,1:T(8,128)(2,1)S(1)} copy-done((bf16[64,8,32]{0,2,1:T(8,128)(2,1)S(1)}, bf16[64,8,32]{0,2,1:T(8,128)(2,1)}, u32[]{:S(2)}) %copy-start.9) | copy-done | bytes 32792
  16.6 0.0 copy-start.10
  16.6 0.7 %copy-done.10 = s32[512,8]{0,1:T(8,128)S(1)} copy-done((s32[512,8]{0,1:T(8,128)S(1)}, s32[512,8]{0,1:T(8,128)}, u32[]{:S(2)}) %copy-start.10) | copy-done | bytes 16408
  17.3 0.0 copy-start.11
  17.3 0.7 %copy-done.11 = s32[512,8]{0,1:T(8,128)S(1)} copy-done((s32[512,8]{0,1:T(8,128)S(1)}, s32[512,8]{0,1:T(8,128)}, u32[]{:S(2)}) %copy-start.11) | copy-done | bytes 16408
  18.0 0.0 copy-start.12
  18.0 0.7 %copy-done.12 = s32[512]{0:T(512)S(1)} copy-done((s32[512]{0:T(512)S(1)}, s32[512]{0:T(512)}, u32[]{:S(2)}) %copy-start.12) | copy-done | bytes 2072
  18.7 1.7 %tables.1 = (bf16[4096,512]{1,0:T(8,128)(2,1)S(1)}, f32[4096,512]{1,0:T(8,128)S(1)}) custom-call(s32[8,512]{1,0:T(8,128)S(1)} %bitcast.12, s32[8,512]{1,0:T(8,128)S(1)} %bitcast.13, s32[1,512]{1,0:T(1,128)S(1)} %bitcast.14, bf16[256,64]{1,0:T(8,128)(2,1)S(1)} %bitcast.11), custom_call_target="tpu_custom_call" | custom-call | flops 268435456 | bytes 12582912 | tf_op jit(solution)/shard_map/tables/pallas_call | solution.py:177
  20.4 0.0 copy-start
  20.4 3.2 %copy-done = f32[4096,512]{1,0:T(8,128)} copy-done((f32[4096,512]{1,0:T(8,128)}, f32[4096,512]{1,0:T(8,128)S(1)}, u32[]{:S(2)}) %copy-start) | copy-done | bytes 8388632
  23.6 0.0 copy-start.2
  23.6 2.0 %copy-done.2 = bf16[4096,512]{1,0:T(8,128)(2,1)} copy-done((bf16[4096,512]{1,0:T(8,128)(2,1)}, bf16[4096,512]{1,0:T(8,128)(2,1)S(1)}, u32[]{:S(2)}) %copy-start.2) | copy-done | bytes 4194328
  25.6 1.5 %all-to-all-done = bf16[128,8,128]{2,1,0:T(8,128)(2,1)S(1)} async-done(((bf16[128,8,128]{2,1,0:T(8,128)(2,1)}), bf16[128,8,128]{2,1,0:T(8,128)(2,1)S(1)}, u32[]{:S(2)}, u32[]{:S(2)}) %all-to-all-start) | async-done | bytes 262176 | tf_op jit(solution)/shard_map/all_to_all | solution.py:175
  27.1 0.0 copy-start.1
  27.1 3.4 %copy-done.1 = f32[4096,512]{1,0:T(8,128)S(1)} copy-done((f32[4096,512]{1,0:T(8,128)S(1)}, f32[4096,512]{1,0:T(8,128)}, u32[]{:S(2)}) %copy-start.1) | copy-done | bytes 8388632
  30.4 0.0 copy-start.3
  30.5 2.2 %copy-done.3 = bf16[4096,512]{1,0:T(8,128)(2,1)S(1)} copy-done((bf16[4096,512]{1,0:T(8,128)(2,1)S(1)}, bf16[4096,512]{1,0:T(8,128)(2,1)}, u32[]{:S(2)}) %copy-start.3) | copy-done | bytes 4194328
  32.6 0.0 copy-start.5
  32.6 1.6 %translate.1 = bf16[32,8,128]{2,1,0:T(8,128)(2,1)S(1)} custom-call(bf16[32,4,8,128]{3,2,1,0:T(8,128)(2,1)S(1)} %bitcast.8, bf16[4096,512]{1,0:T(8,128)(2,1)S(1)} %copy-done.3, f32[4096,512]{1,0:T(8,128)S(1)} %copy-done.1), custom_call_target="tpu_custom_call" | custom-call | tf_op jit(solution)/shard_map/translate/pallas_call | solution.py:198
  34.2 13.5 %all_to_all.10.rays_ref = bf16[32,8,128]{2,1,0:T(8,128)(2,1)S(1)} all-to-all(bf16[32,8,128]{2,1,0:T(8,128)(2,1)S(1)} %translate.1), channel_id=1, replica_groups=mesh['dom'=32,'tm'=4] {'dom'}, dimensions={0} | all-to-all | bytes 131072 | tf_op jit(solution)/shard_map/all_to_all | solution.py:212
  47.8 0.0 copy-done.5
  47.8 0.0 copy-done.7
  47.8 1.4 %receive.1 = bf16[2,1024]{1,0:T(2,128)(2,1)} custom-call(bf16[32,8,128]{2,1,0:T(8,128)(2,1)S(1)} %all_to_all.10.rays_ref, s32[1,1024]{1,0:T(1,128)S(1)} %bitcast.10, bf16[1024,1024]{1,0:T(8,128)(2,1)S(1)} %copy-done.5), custom_call_target="tpu_custom_call" | custom-call | tf_op jit(solution)/shard_map/receive/pallas_call | solution.py:213
  (1 shorter events, 0.0 us)
Async XLA Ops:
  0.0 1.6 %copy-start.4 = (bf16[1024,1024]{1,0:T(8,128)(2,1)S(1)}, bf16[1024,1024]{1,0:T(8,128)(2,1)}, u32[]{:S(2)}) copy-start(bf16[1024,1024]{1,0:T(8,128)(2,1)} %radiation_ref.1) | copy-start | bytes 6291460
  1.6 0.7 %copy-start.6 = (s32[1024]{0:T(1024)S(1)}, s32[1024]{0:T(1024)}, u32[]{:S(2)}) copy-start(s32[1024]{0:T(1024)} %param.9) | copy-start | bytes 12292
  2.3 0.7 %copy-start.8 = (bf16[2,1024]{1,0:T(2,128)(2,1)S(1)}, bf16[2,1024]{1,0:T(2,128)(2,1)}, u32[]{:S(2)}) copy-start(bf16[2,1024]{1,0:T(2,128)(2,1)} %signal_ref.1) | copy-start | bytes 12292
  4.2 22.8 %all-to-all-start = ((bf16[128,8,128]{2,1,0:T(8,128)(2,1)}), bf16[128,8,128]{2,1,0:T(8,128)(2,1)S(1)}, u32[]{:S(2)}, u32[]{:S(2)}) async-start(bf16[128,8,128]{2,1,0:T(8,128)(2,1)} %aggregate.1), calls=%async_computation | async-start | bytes 524288 | tf_op jit(solution)/shard_map/all_to_all | solution.py:175
  15.7 0.8 %copy-start.9 = (bf16[64,8,32]{0,2,1:T(8,128)(2,1)S(1)}, bf16[64,8,32]{0,2,1:T(8,128)(2,1)}, u32[]{:S(2)}) copy-start(bf16[64,8,32]{0,2,1:T(8,128)(2,1)} %param.12) | copy-start | bytes 98308
  16.6 0.7 %copy-start.10 = (s32[512,8]{0,1:T(8,128)S(1)}, s32[512,8]{0,1:T(8,128)}, u32[]{:S(2)}) copy-start(s32[512,8]{0,1:T(8,128)} %param.13) | copy-start | bytes 49156
  17.3 0.7 %copy-start.11 = (s32[512,8]{0,1:T(8,128)S(1)}, s32[512,8]{0,1:T(8,128)}, u32[]{:S(2)}) copy-start(s32[512,8]{0,1:T(8,128)} %param.14) | copy-start | bytes 49156
  18.0 0.7 %copy-start.12 = (s32[512]{0:T(512)S(1)}, s32[512]{0:T(512)}, u32[]{:S(2)}) copy-start(s32[512]{0:T(512)} %param.15) | copy-start | bytes 6148
  20.4 3.2 %copy-start = (f32[4096,512]{1,0:T(8,128)}, f32[4096,512]{1,0:T(8,128)S(1)}, u32[]{:S(2)}) copy-start(f32[4096,512]{1,0:T(8,128)S(1)} %get-tuple-element.8.weight_ref) | copy-start | bytes 25165828
  23.6 2.0 %copy-start.2 = (bf16[4096,512]{1,0:T(8,128)(2,1)}, bf16[4096,512]{1,0:T(8,128)(2,1)S(1)}, u32[]{:S(2)}) copy-start(bf16[4096,512]{1,0:T(8,128)(2,1)S(1)} %get-tuple-element.7.pick_ref) | copy-start | bytes 12582916
  27.1 3.4 %copy-start.1 = (f32[4096,512]{1,0:T(8,128)S(1)}, f32[4096,512]{1,0:T(8,128)}, u32[]{:S(2)}) copy-start(f32[4096,512]{1,0:T(8,128)} %copy-done) | copy-start | bytes 25165828
  30.4 2.2 %copy-start.3 = (bf16[4096,512]{1,0:T(8,128)(2,1)S(1)}, bf16[4096,512]{1,0:T(8,128)(2,1)}, u32[]{:S(2)}) copy-start(bf16[4096,512]{1,0:T(8,128)(2,1)} %copy-done.2) | copy-start | bytes 12582916
  32.6 15.1 %copy-start.5 = (bf16[1024,1024]{1,0:T(8,128)(2,1)S(1)}, bf16[1024,1024]{1,0:T(8,128)(2,1)}, u32[]{:S(2)}) copy-start(bf16[1024,1024]{1,0:T(8,128)(2,1)} %reception_ref.1) | copy-start | bytes 6291460
  32.6 15.1 %copy-start.7 = (s32[1024]{0:T(1024)S(1)}, s32[1024]{0:T(1024)}, u32[]{:S(2)}) copy-start(s32[1024]{0:T(1024)} %param.9) | copy-start | bytes 12292

commit v2 on v1

--- a/solution.py
+++ b/solution.py
@@ -18,7 +18,9 @@
 GROUPS = K // 128
 CHUNK = 128
 N_CHUNK = BOXES // CHUNK
+N_LOAD = 4
 VMEM = pl.BlockSpec(memory_space=pltpu.VMEM)
+HBM = pl.BlockSpec(memory_space=pltpu.HBM)
 
 
 def owner_rows(box_ref, half):
@@ -30,7 +32,48 @@
     return lax.broadcasted_iota(jnp.int32, shape, len(shape) - 1) // DIRS
 
 
-def aggregate_kernel(signal_ref, box_ref, radiation_ref, out_ref):
+def aggregate_kernel(
+    signal_hbm, box_hbm, radiation_hbm, source_hbm, class_hbm, count_hbm,
+    out_ref, pick_ref, hot_ref,
+    signal_ref, box_ref, radiation_ref, source_ref, class_ref, count_ref, sems,
+):
+    small = [
+        (source_hbm, source_ref),
+        (class_hbm, class_ref),
+        (count_hbm, count_ref),
+        (signal_hbm, signal_ref),
+        (box_hbm, box_ref),
+    ]
+    copies = [pltpu.make_async_copy(src, dst, sems.at[i]) for i, (src, dst) in enumerate(small)]
+    height = PAN_DEV // N_LOAD
+    for part in range(N_LOAD):
+        rows = pl.ds(part * height, height)
+        copies.append(
+            pltpu.make_async_copy(
+                radiation_hbm.at[rows], radiation_ref.at[rows], sems.at[len(small) + part]
+            )
+        )
+    for copy in copies:
+        copy.start()
+
+    for copy in copies[:3]:
+        copy.wait()
+    used = lax.broadcasted_iota(jnp.int32, (J, BOXES), 0) < count_ref[...]
+    classes = jnp.transpose(jnp.where(used, class_ref[...], -1))
+    sources = jnp.transpose(source_ref[...])
+    lane_s = lax.broadcasted_iota(jnp.int32, (CHUNK, BOXES), 1)
+    lane_c = lax.broadcasted_iota(jnp.int32, (CHUNK, CLASSES), 1)
+    for chunk in range(N_CHUNK):
+        for j in range(J):
+            rows = slice(chunk * CHUNK, chunk * CHUNK + CHUNK)
+            at = pl.ds((chunk * J + j) * CHUNK, CHUNK)
+            src = sources[rows, j : j + 1]
+            cls = classes[rows, j : j + 1]
+            pick_ref[at, :] = (src == lane_s).astype(jnp.float32).astype(jnp.bfloat16)
+            hot_ref[at, :] = (cls == lane_c).astype(jnp.float32).astype(jnp.bfloat16)
+
+    for copy in copies[3:5]:
+        copy.wait()
     signal = signal_ref[...].astype(jnp.float32)
     parts = []
     for half in range(2):
@@ -38,7 +81,13 @@
         for step in range(2):
             parts.append(jnp.where(mine, signal[step : step + 1, :], 0.0))
     masked = jnp.concatenate(parts, axis=0).astype(jnp.bfloat16)
-    rays = jnp.dot(masked, radiation_ref[...], preferred_element_type=jnp.float32)
+    rays = jnp.zeros((32, K), jnp.float32)
+    for part in range(N_LOAD):
+        copies[5 + part].wait()
+        rows = slice(part * height, part * height + height)
+        rays = rays + jnp.dot(
+            masked[:, rows], radiation_ref[rows, :], preferred_element_type=jnp.float32
+        )
     group = lane_group((8, 128))
     for column in range(GROUPS):
         block = [rays[q * 8 : q * 8 + 8, column * 128 : column * 128 + 128] for q in range(4)]
@@ -53,7 +102,9 @@
                 out_ref[(column * 4 + g) * N_TM + plane] = tile
 
 
-def tables_kernel(source_ref, class_ref, count_ref, table_ref, pick_ref, weight_ref, rhs_ref):
+def translate_kernel(
+    rays_ref, pick_ref, hot_ref, table_ref, out_ref, near_ref, rhs_ref, weight_ref, got_ref, sum_ref
+):
     first = lax.axis_index("tm") * 2
     for step_out in range(2):
         for step_in in range(LAGS):
@@ -62,28 +113,6 @@
             rows = table_ref[pl.ds(start, DIRS), :]
             rows = jnp.where(lag >= 0, rows, jnp.zeros_like(rows))
             rhs_ref[pl.ds((step_out * LAGS + step_in) * DIRS, DIRS), :] = rows
-    sources = source_ref[...]
-    used = lax.broadcasted_iota(jnp.int32, (J, BOXES), 0) < count_ref[...]
-    classes = jnp.where(used, class_ref[...], -1)
-    sources = jnp.transpose(sources)
-    classes = jnp.transpose(classes)
-    lane_s = lax.broadcasted_iota(jnp.int32, (CHUNK, BOXES), 1)
-    lane_c = lax.broadcasted_iota(jnp.int32, (CHUNK, CLASSES), 1)
-    rhs = rhs_ref[...]
-    for chunk in range(N_CHUNK):
-        for j in range(J):
-            rows = slice(chunk * CHUNK, chunk * CHUNK + CHUNK)
-            at = pl.ds((chunk * J + j) * CHUNK, CHUNK)
-            src = sources[rows, j : j + 1]
-            cls = classes[rows, j : j + 1]
-            pick_ref[at, :] = (src == lane_s).astype(jnp.float32).astype(jnp.bfloat16)
-            hot = (cls == lane_c).astype(jnp.float32).astype(jnp.bfloat16)
-            weight_ref[at, :] = lax.dot_general(
-                hot, rhs, (((1,), (1,)), ((), ())), preferred_element_type=jnp.float32
-            )
-
-
-def translate_kernel(rays_ref, pick_ref, weight_ref, out_ref, near_ref, got_ref, sum_ref):
     low = lax.broadcasted_iota(jnp.int32, (N_DOM, 8, 128), 2) < 64
     for pair in range(2):
         left = rays_ref[:, 2 * pair].astype(jnp.float32)
@@ -95,20 +124,25 @@
     rows_chunk = J * CHUNK
     for chunk in range(N_CHUNK):
         base = chunk * rows_chunk
-        got_ref[...] = jnp.dot(
-            pick_ref[base : base + rows_chunk, :],
-            near_ref[...],
+        rows = slice(base, base + rows_chunk)
+        weight_ref[rows, :] = lax.dot_general(
+            hot_ref[rows, :],
+            rhs_ref[...],
+            (((1,), (1,)), ((), ())),
             preferred_element_type=jnp.float32,
+        )
+        got_ref[rows, :] = jnp.dot(
+            pick_ref[rows, :], near_ref[...], preferred_element_type=jnp.float32
         )
         for piece in range(CHUNK // 16):
             total = [jnp.zeros((16, 128), jnp.float32) for _ in range(2)]
             for j in range(J):
-                at = j * CHUNK + piece * 16
+                at = base + j * CHUNK + piece * 16
                 for side in range(2):
                     got = got_ref[at : at + 16, side * 128 : side * 128 + 128]
                     for step in range(2):
                         lanes = slice(step * 256 + side * 128, step * 256 + side * 128 + 128)
-                        total[step] = total[step] + weight_ref[base + at : base + at + 16, lanes] * got
+                        total[step] = total[step] + weight_ref[at : at + 16, lanes] * got
             for step in range(2):
                 at = chunk * CHUNK + piece * 16
                 sum_ref[at : at + 16, step * 128 : step * 128 + 128] = total[step]
@@ -156,6 +190,10 @@
     out_ref[...] = jnp.concatenate(steps, axis=0).astype(jnp.bfloat16)
 
 
+def in_hbm(array):
+    return pltpu.with_memory_space_constraint(array, pltpu.HBM)
+
+
 def params(mib):
     return pltpu.CompilerParams(vmem_limit_bytes=mib << 20)
 
@@ -164,50 +202,56 @@
     panel_signal, panel_box, radiation, reception, translation, list_source, list_class, list_count
 ):
     boxes_row = panel_box.reshape(1, PAN_DEV)
-    blocks = pl.pallas_call(
+    blocks, pick, hot = pl.pallas_call(
         aggregate_kernel,
-        out_shape=jax.ShapeDtypeStruct((N_DOM * N_TM, 8, 128), jnp.bfloat16),
-        in_specs=[VMEM] * 3,
-        out_specs=VMEM,
-        compiler_params=params(16),
+        out_shape=(
+            jax.ShapeDtypeStruct((N_DOM * N_TM, 8, 128), jnp.bfloat16),
+            jax.ShapeDtypeStruct((BOXES * J, BOXES), jnp.bfloat16),
+            jax.ShapeDtypeStruct((BOXES * J, CLASSES), jnp.bfloat16),
+        ),
+        in_specs=[HBM] * 6,
+        out_specs=(VMEM,) * 3,
+        scratch_shapes=[
+            pltpu.VMEM((2, PAN_DEV), jnp.bfloat16),
+            pltpu.VMEM((1, PAN_DEV), jnp.int32),
+            pltpu.VMEM((PAN_DEV, K), jnp.bfloat16),
+            pltpu.VMEM((J, BOXES), jnp.int32),
+            pltpu.VMEM((J, BOXES), jnp.int32),
+            pltpu.VMEM((1, BOXES), jnp.int32),
+            pltpu.SemaphoreType.DMA((5 + N_LOAD,)),
+        ],
+        compiler_params=params(40),
         name="aggregate",
-    )(panel_signal, boxes_row, radiation)
+    )(
+        in_hbm(panel_signal),
+        in_hbm(boxes_row),
+        in_hbm(radiation),
+        in_hbm(list_source.T),
+        in_hbm(list_class.T),
+        in_hbm(list_count.reshape(1, BOXES)),
+    )
     spread = lax.all_to_all(blocks, ("dom", "tm"), split_axis=0, concat_axis=0, tiled=True)
-
-    pick, weight = pl.pallas_call(
-        tables_kernel,
-        out_shape=(
-            jax.ShapeDtypeStruct((BOXES * J, BOXES), jnp.bfloat16),
-            jax.ShapeDtypeStruct((BOXES * J, 2 * LAGS * DIRS), jnp.float32),
-        ),
-        in_specs=[VMEM] * 4,
-        out_specs=(VMEM, VMEM),
-        scratch_shapes=[pltpu.VMEM((2 * LAGS * DIRS, CLASSES), jnp.bfloat16)],
-        compiler_params=params(32),
-        cost_estimate=pl.CostEstimate(
-            flops=2 * 4096 * 64 * 512, bytes_accessed=12 << 20, transcendentals=0
-        ),
-        name="tables",
-    )(
-        list_source.T,
-        list_class.T,
-        list_count.reshape(1, BOXES),
-        jnp.transpose(translation, (1, 2, 0)).reshape(LAGS * DIRS, CLASSES),
-    )
 
     incoming = pl.pallas_call(
         translate_kernel,
         out_shape=jax.ShapeDtypeStruct((N_DOM, 8, 128), jnp.bfloat16),
-        in_specs=[VMEM] * 3,
+        in_specs=[VMEM] * 4,
         out_specs=VMEM,
         scratch_shapes=[
             pltpu.VMEM((BOXES, 256), jnp.bfloat16),
-            pltpu.VMEM((J * CHUNK, 256), jnp.float32),
+            pltpu.VMEM((2 * LAGS * DIRS, CLASSES), jnp.bfloat16),
+            pltpu.VMEM((BOXES * J, 512), jnp.float32),
+            pltpu.VMEM((BOXES * J, 256), jnp.float32),
             pltpu.VMEM((BOXES, 256), jnp.float32),
         ],
-        compiler_params=params(32),
+        compiler_params=params(40),
         name="translate",
-    )(spread.reshape(N_DOM, N_TM, 8, 128), pick, weight)
+    )(
+        spread.reshape(N_DOM, N_TM, 8, 128),
+        pick,
+        hot,
+        jnp.transpose(translation, (1, 2, 0)).reshape(LAGS * DIRS, CLASSES),
+    )
 
     rays = lax.all_to_all(incoming, "dom", split_axis=0, concat_axis=0, tiled=True)
     return pl.pallas_call(

time: 49.7 us -> 40.9 us (0.82)
  blocking collectives: 13.5 us -> 33.8 us
  local copies, waits for them, and re-layouts: 16.7 us -> 0.01 us
  starting transfers between devices: 11.5 us -> 0 us
  waiting for transfers between devices: 1.5 us -> 0 us
  Pallas kernels: 5.89 us -> 6.88 us
    all_to_all x0 -> x1, blocking collectives: none -> 22.6 us  [body(): lax.all_to_all(blocks, ('dom', 'tm'), split_axis=0, concat_axis=0, tiled=...]
    unnamed x26 -> x6, local copies, waits for them, and re-layouts: 16.7 us -> 0.01 us
    all_to_all x1 -> x0, starting transfers between devices: 11.5 us -> none  [body(): lax.all_to_all(blocks, ('dom', 'tm'), split_axis=0, concat_axis=0, tiled=...]
    all_to_all x1, blocking collectives: 13.5 us -> 11.2 us  [body(): lax.all_to_all(incoming, 'dom', split_axis=0, concat_axis=0, tiled=True)]
    all_to_all x1 -> x0, waiting for transfers between devices: 1.5 us -> none  [body(): lax.all_to_all(blocks, ('dom', 'tm'), split_axis=0, concat_axis=0, tiled=...]
    pallas_call x1, Pallas kernels: 1.58 us -> 2.59 us  [body(): pl.pallas_call(translate_kernel, out_shape=jax.ShapeDtypeStruct((N_DOM, 8...]
    pallas_call x2 -> x1, Pallas kernels: 2.95 us -> 2.93 us  [body(): pl.pallas_call(aggregate_kernel, out_shape=(jax.ShapeDtypeStruct((N_DOM *...]
  transfers between devices with their start and end apart: 1 -> 0, of which waited for: 1 -> 0; matrix products, arithmetic and copies ran while one was open for 0% -> 0% of each run, Pallas kernels for 3% -> 0%
where the time goes in v2:
time: 40.9 us; the launch traced here: 40.7 us
  blocking collectives  33.8 us (83%)
  Pallas kernels  6.88 us (17%)
    all_to_all x1, blocking collectives, body(): lax.all_to_all(blocks, ('dom', 'tm'), split_axis=0, concat_axis=0, tiled=...  22.6 us
    all_to_all x1, blocking collectives, body(): lax.all_to_all(incoming, 'dom', split_axis=0, concat_axis=0, tiled=True)  11.2 us
    pallas_call x1, Pallas kernels, body(): pl.pallas_call(aggregate_kernel, out_shape=(jax.ShapeDtypeStruct((N_DOM *...  2.93 us
    pallas_call x1, Pallas kernels, body(): pl.pallas_call(translate_kernel, out_shape=jax.ShapeDtypeStruct((N_DOM, 8...  2.59 us
    pallas_call x1, Pallas kernels, body(): pl.pallas_call(receive_kernel, out_shape=jax.ShapeDtypeStruct((2, PAN_DEV...  1.36 us

profile of v2, /device:TPU:1, one launch (start us, length us, event | category | flops | bytes accessed | tf_op | source)
XLA Modules:
  0.0 40.7 jit_solution(16365225466545461806)
XLA Ops:
  0.0 0.0 copy-start.1
  0.0 2.9 %aggregate.1 = (bf16[128,8,128]{2,1,0:T(8,128)(2,1)S(1)}, bf16[4096,512]{1,0:T(8,128)(2,1)S(1)}, bf16[4096,64]{1,0:T(8,128)(2,1)S(1)}) custom-call(bf16[2,1024]{1,0:T(2,128)(2,1)} %signal_hbm.1, s32[1,1024]{1,0:T(1,128)} %bitcast.10, bf16[1024,1024]{1,0:T(8,128)(2,1)} %radiation_hbm.1, s32[8,512]{1,0:T(8,128)} %bitcast.12, s32[8,512]{1,0:T(8,128)} %bitcast.13, ...), custom_call_target="tpu_custom_call" | custom-call | tf_op jit(solution)/shard_map/aggregate/pallas_call | solution.py:205
  2.9 22.6 %all_to_all.10 = bf16[128,8,128]{2,1,0:T(8,128)(2,1)S(1)} all-to-all(bf16[128,8,128]{2,1,0:T(8,128)(2,1)S(1)} %get-tuple-element.8), channel_id=1, replica_groups=mesh['dom'=32,'tm'=4] {'dom','tm'}, dimensions={0} | all-to-all | bytes 524288 | tf_op jit(solution)/shard_map/all_to_all | solution.py:233
  25.6 0.0 copy-done.1
  25.6 0.0 copy-start
  25.6 0.0 copy-start.2
  25.6 2.6 %translate.1 = bf16[32,8,128]{2,1,0:T(8,128)(2,1)S(1)} custom-call(bf16[32,4,8,128]{3,2,1,0:T(8,128)(2,1)S(1)} %bitcast.8, bf16[4096,512]{1,0:T(8,128)(2,1)S(1)} %get-tuple-element.9.pick_ref, bf16[4096,64]{1,0:T(8,128)(2,1)S(1)} %get-tuple-element.10.hot_ref, bf16[256,64]{1,0:T(8,128)(2,1)S(1)} %bitcast.9), custom_call_target="tpu_custom_call" | custom-call | tf_op jit(solution)/shard_map/translate/pallas_call | solution.py:235
  28.2 11.2 %all_to_all.11.rays_ref = bf16[32,8,128]{2,1,0:T(8,128)(2,1)S(1)} all-to-all(bf16[32,8,128]{2,1,0:T(8,128)(2,1)S(1)} %translate.1), channel_id=1, replica_groups=mesh['dom'=32,'tm'=4] {'dom'}, dimensions={0} | all-to-all | bytes 131072 | tf_op jit(solution)/shard_map/all_to_all | solution.py:256
  39.4 0.0 copy-done
  39.4 0.0 copy-done.2
  39.4 1.4 %receive.1 = bf16[2,1024]{1,0:T(2,128)(2,1)} custom-call(bf16[32,8,128]{2,1,0:T(8,128)(2,1)S(1)} %all_to_all.11.rays_ref, s32[1,1024]{1,0:T(1,128)S(1)} %bitcast.11, bf16[1024,1024]{1,0:T(8,128)(2,1)S(1)} %copy-done), custom_call_target="tpu_custom_call" | custom-call | tf_op jit(solution)/shard_map/receive/pallas_call | solution.py:257
Async XLA Ops:
  0.0 25.6 %copy-start.1 = (bf16[64,8,32]{0,2,1:T(8,128)(2,1)S(1)}, bf16[64,8,32]{0,2,1:T(8,128)(2,1)}, u32[]{:S(2)}) copy-start(bf16[64,8,32]{0,2,1:T(8,128)(2,1)} %param.12) | copy-start | bytes 98308
  25.6 13.8 %copy-start = (bf16[1024,1024]{1,0:T(8,128)(2,1)S(1)}, bf16[1024,1024]{1,0:T(8,128)(2,1)}, u32[]{:S(2)}) copy-start(bf16[1024,1024]{1,0:T(8,128)(2,1)} %reception_ref.1) | copy-start | bytes 6291460
  25.6 13.8 %copy-start.2 = (s32[1024]{0:T(1024)S(1)}, s32[1024]{0:T(1024)}, u32[]{:S(2)}) copy-start(s32[1024]{0:T(1024)} %param.9) | copy-start | bytes 12292

commit v3 on v1

--- a/solution.py
+++ b/solution.py
@@ -19,6 +19,7 @@
 CHUNK = 128
 N_CHUNK = BOXES // CHUNK
 VMEM = pl.BlockSpec(memory_space=pltpu.VMEM)
+HBM = pl.BlockSpec(memory_space=pltpu.HBM)
 
 
 def owner_rows(box_ref, half):
@@ -30,46 +31,44 @@
     return lax.broadcasted_iota(jnp.int32, shape, len(shape) - 1) // DIRS
 
 
-def aggregate_kernel(signal_ref, box_ref, radiation_ref, out_ref):
-    signal = signal_ref[...].astype(jnp.float32)
+def tables_kernel(
+    source_hbm, class_hbm, count_hbm, table_hbm, signal_hbm, box_hbm, radiation_hbm,
+    pick_ref, weight_ref, signal_ref, box_ref, radiation_ref,
+    source_ref, class_ref, count_ref, table_ref, sems,
+):
+    pairs = [
+        (source_hbm, source_ref),
+        (class_hbm, class_ref),
+        (count_hbm, count_ref),
+        (table_hbm, table_ref),
+        (signal_hbm, signal_ref),
+        (box_hbm, box_ref),
+        (radiation_hbm, radiation_ref),
+    ]
+    copies = [pltpu.make_async_copy(src, dst, sems.at[i]) for i, (src, dst) in enumerate(pairs)]
+    for copy in copies:
+        copy.start()
+    for copy in copies[:4]:
+        copy.wait()
+    plane = lax.axis_index("tm")
+    table = table_ref[...]
+    blank = jnp.zeros((DIRS, CLASSES), jnp.bfloat16)
     parts = []
-    for half in range(2):
-        mine = owner_rows(box_ref, half)
-        for step in range(2):
-            parts.append(jnp.where(mine, signal[step : step + 1, :], 0.0))
-    masked = jnp.concatenate(parts, axis=0).astype(jnp.bfloat16)
-    rays = jnp.dot(masked, radiation_ref[...], preferred_element_type=jnp.float32)
-    group = lane_group((8, 128))
-    for column in range(GROUPS):
-        block = [rays[q * 8 : q * 8 + 8, column * 128 : column * 128 + 128] for q in range(4)]
-        for g in range(4):
-            tile = None
-            for q in range(4):
-                turn = ((q - g) % 4) * DIRS
-                moved = block[q] if turn == 0 else pltpu.roll(block[q], turn, 1)
-                tile = moved if tile is None else jnp.where(group == q, moved, tile)
-            tile = tile.astype(jnp.bfloat16)
-            for plane in range(N_TM):
-                out_ref[(column * 4 + g) * N_TM + plane] = tile
-
-
-def tables_kernel(source_ref, class_ref, count_ref, table_ref, pick_ref, weight_ref, rhs_ref):
-    first = lax.axis_index("tm") * 2
     for step_out in range(2):
-        for step_in in range(LAGS):
-            lag = first + step_out - step_in
-            start = pl.multiple_of(jnp.maximum(lag, 0) * DIRS, DIRS)
-            rows = table_ref[pl.ds(start, DIRS), :]
-            rows = jnp.where(lag >= 0, rows, jnp.zeros_like(rows))
-            rhs_ref[pl.ds((step_out * LAGS + step_in) * DIRS, DIRS), :] = rows
-    sources = source_ref[...]
+        for back in range(N_TM):
+            for step_in in range(2):
+                lag = 2 * back + step_out - step_in
+                if lag < 0:
+                    parts.append(blank)
+                    continue
+                rows = table[lag * DIRS : lag * DIRS + DIRS, :]
+                parts.append(jnp.where(plane >= back, rows, blank))
+    rhs = jnp.concatenate(parts, axis=0)
     used = lax.broadcasted_iota(jnp.int32, (J, BOXES), 0) < count_ref[...]
-    classes = jnp.where(used, class_ref[...], -1)
-    sources = jnp.transpose(sources)
-    classes = jnp.transpose(classes)
+    classes = jnp.transpose(jnp.where(used, class_ref[...], -1))
+    sources = jnp.transpose(source_ref[...])
     lane_s = lax.broadcasted_iota(jnp.int32, (CHUNK, BOXES), 1)
     lane_c = lax.broadcasted_iota(jnp.int32, (CHUNK, CLASSES), 1)
-    rhs = rhs_ref[...]
     for chunk in range(N_CHUNK):
         for j in range(J):
             rows = slice(chunk * CHUNK, chunk * CHUNK + CHUNK)
@@ -81,6 +80,32 @@
             weight_ref[at, :] = lax.dot_general(
                 hot, rhs, (((1,), (1,)), ((), ())), preferred_element_type=jnp.float32
             )
+    for copy in copies[4:]:
+        copy.wait()
+
+
+def aggregate_kernel(own_ref, one_ref, two_ref, three_ref, box_ref, radiation_ref, out_ref):
+    mine = [owner_rows(box_ref, half) for half in range(2)]
+    parts = []
+    for ref in (own_ref, one_ref, two_ref, three_ref):
+        signal = ref[...].astype(jnp.float32)
+        for half in range(2):
+            for step in range(2):
+                parts.append(jnp.where(mine[half], signal[step : step + 1, :], 0.0))
+    masked = jnp.concatenate(parts, axis=0).astype(jnp.bfloat16)
+    rays = jnp.dot(masked, radiation_ref[...], preferred_element_type=jnp.float32)
+    group = lane_group((8, 128))
+    for back in range(N_TM):
+        for column in range(GROUPS):
+            lanes = slice(column * 128, column * 128 + 128)
+            block = [rays[(back * 4 + q) * 8 : (back * 4 + q) * 8 + 8, lanes] for q in range(4)]
+            for g in range(4):
+                tile = None
+                for q in range(4):
+                    turn = ((q - g) % 4) * DIRS
+                    moved = block[q] if turn == 0 else pltpu.roll(block[q], turn, 1)
+                    tile = moved if tile is None else jnp.where(group == q, moved, tile)
+                out_ref[(column * 4 + g) * N_TM + back] = tile.astype(jnp.bfloat16)
 
 
 def translate_kernel(rays_ref, pick_ref, weight_ref, out_ref, near_ref, got_ref, sum_ref):
@@ -95,20 +120,19 @@
     rows_chunk = J * CHUNK
     for chunk in range(N_CHUNK):
         base = chunk * rows_chunk
-        got_ref[...] = jnp.dot(
-            pick_ref[base : base + rows_chunk, :],
-            near_ref[...],
-            preferred_element_type=jnp.float32,
+        rows = slice(base, base + rows_chunk)
+        got_ref[rows, :] = jnp.dot(
+            pick_ref[rows, :], near_ref[...], preferred_element_type=jnp.float32
         )
         for piece in range(CHUNK // 16):
             total = [jnp.zeros((16, 128), jnp.float32) for _ in range(2)]
             for j in range(J):
-                at = j * CHUNK + piece * 16
+                at = base + j * CHUNK + piece * 16
                 for side in range(2):
                     got = got_ref[at : at + 16, side * 128 : side * 128 + 128]
                     for step in range(2):
                         lanes = slice(step * 256 + side * 128, step * 256 + side * 128 + 128)
-                        total[step] = total[step] + weight_ref[base + at : base + at + 16, lanes] * got
+                        total[step] = total[step] + weight_ref[at : at + 16, lanes] * got
             for step in range(2):
                 at = chunk * CHUNK + piece * 16
                 sum_ref[at : at + 16, step * 128 : step * 128 + 128] = total[step]
@@ -156,6 +180,10 @@
     out_ref[...] = jnp.concatenate(steps, axis=0).astype(jnp.bfloat16)
 
 
+def in_hbm(array):
+    return pltpu.with_memory_space_constraint(array, pltpu.HBM)
+
+
 def params(mib):
     return pltpu.CompilerParams(vmem_limit_bytes=mib << 20)
 
@@ -164,36 +192,51 @@
     panel_signal, panel_box, radiation, reception, translation, list_source, list_class, list_count
 ):
     boxes_row = panel_box.reshape(1, PAN_DEV)
-    blocks = pl.pallas_call(
-        aggregate_kernel,
-        out_shape=jax.ShapeDtypeStruct((N_DOM * N_TM, 8, 128), jnp.bfloat16),
-        in_specs=[VMEM] * 3,
-        out_specs=VMEM,
-        compiler_params=params(16),
-        name="aggregate",
-    )(panel_signal, boxes_row, radiation)
-    spread = lax.all_to_all(blocks, ("dom", "tm"), split_axis=0, concat_axis=0, tiled=True)
-
-    pick, weight = pl.pallas_call(
+    earlier = [
+        lax.ppermute(panel_signal, "tm", [(p, (p + back) % N_TM) for p in range(N_TM)])
+        for back in range(1, N_TM)
+    ]
+    pick, weight, own_signal, own_box, own_radiation = pl.pallas_call(
         tables_kernel,
         out_shape=(
             jax.ShapeDtypeStruct((BOXES * J, BOXES), jnp.bfloat16),
             jax.ShapeDtypeStruct((BOXES * J, 2 * LAGS * DIRS), jnp.float32),
+            jax.ShapeDtypeStruct((2, PAN_DEV), jnp.bfloat16),
+            jax.ShapeDtypeStruct((1, PAN_DEV), jnp.int32),
+            jax.ShapeDtypeStruct((PAN_DEV, K), jnp.bfloat16),
         ),
-        in_specs=[VMEM] * 4,
-        out_specs=(VMEM, VMEM),
-        scratch_shapes=[pltpu.VMEM((2 * LAGS * DIRS, CLASSES), jnp.bfloat16)],
+        in_specs=[HBM] * 7,
+        out_specs=(VMEM,) * 5,
+        scratch_shapes=[
+            pltpu.VMEM((J, BOXES), jnp.int32),
+            pltpu.VMEM((J, BOXES), jnp.int32),
+            pltpu.VMEM((1, BOXES), jnp.int32),
+            pltpu.VMEM((LAGS * DIRS, CLASSES), jnp.bfloat16),
+            pltpu.SemaphoreType.DMA((7,)),
+        ],
         compiler_params=params(32),
         cost_estimate=pl.CostEstimate(
             flops=2 * 4096 * 64 * 512, bytes_accessed=12 << 20, transcendentals=0
         ),
         name="tables",
     )(
-        list_source.T,
-        list_class.T,
-        list_count.reshape(1, BOXES),
-        jnp.transpose(translation, (1, 2, 0)).reshape(LAGS * DIRS, CLASSES),
-    )
+        in_hbm(list_source.T),
+        in_hbm(list_class.T),
+        in_hbm(list_count.reshape(1, BOXES)),
+        in_hbm(jnp.transpose(translation, (1, 2, 0)).reshape(LAGS * DIRS, CLASSES)),
+        in_hbm(panel_signal),
+        in_hbm(boxes_row),
+        in_hbm(radiation),
+    )
+    blocks = pl.pallas_call(
+        aggregate_kernel,
+        out_shape=jax.ShapeDtypeStruct((N_DOM * N_TM, 8, 128), jnp.bfloat16),
+        in_specs=[VMEM] * 6,
+        out_specs=VMEM,
+        compiler_params=params(16),
+        name="aggregate",
+    )(own_signal, *earlier, own_box, own_radiation)
+    spread = lax.all_to_all(blocks, "dom", split_axis=0, concat_axis=0, tiled=True)
 
     incoming = pl.pallas_call(
         translate_kernel,
@@ -202,7 +245,7 @@
         out_specs=VMEM,
         scratch_shapes=[
             pltpu.VMEM((BOXES, 256), jnp.bfloat16),
-            pltpu.VMEM((J * CHUNK, 256), jnp.float32),
+            pltpu.VMEM((BOXES * J, 256), jnp.float32),
             pltpu.VMEM((BOXES, 256), jnp.float32),
         ],
         compiler_params=params(32),
@@ -217,7 +260,7 @@
         out_specs=VMEM,
         compiler_params=params(16),
         name="receive",
-    )(rays, boxes_row, reception)
+    )(rays, own_box, reception)
 
 
 def solution(mesh):

time: 49.7 us -> 41.6 us (0.84)
  local copies, waits for them, and re-layouts: 16.7 us -> 0.01 us
  blocking collectives: 13.5 us -> 30.1 us
  starting transfers between devices: 11.5 us -> 5.04 us
  waiting for transfers between devices: 1.5 us -> 0.01 us
    all_to_all x0 -> x1, blocking collectives: none -> 19.2 us  [body(): lax.all_to_all(blocks, 'dom', split_axis=0, concat_axis=0, tiled=True)]
    unnamed x26 -> x2, local copies, waits for them, and re-layouts: 16.7 us -> 0.01 us
    all_to_all x1 -> x0, starting transfers between devices: 11.5 us -> none  [body(): lax.all_to_all(blocks, ('dom', 'tm'), split_axis=0, concat_axis=0, tiled=...]
    ppermute x0 -> x3, starting transfers between devices: none -> 5.04 us  [body(): lax.ppermute(panel_signal, 'tm', [(p, (p + back) % N_TM) for p in range(N...]
    all_to_all x1, blocking collectives: 13.5 us -> 10.8 us  [body(): lax.all_to_all(incoming, 'dom', split_axis=0, concat_axis=0, tiled=True)]
    all_to_all x1 -> x0, waiting for transfers between devices: 1.5 us -> none  [body(): lax.all_to_all(blocks, ('dom', 'tm'), split_axis=0, concat_axis=0, tiled=...]
    pallas_call x1, Pallas kernels: 1.68 us -> 2.63 us  [body(): pl.pallas_call(tables_kernel, out_shape=(jax.ShapeDtypeStruct((BOXES * J,...]
    pallas_call x1, Pallas kernels: 1.27 us -> 0.6 us  [body(): pl.pallas_call(aggregate_kernel, out_shape=jax.ShapeDtypeStruct((N_DOM *...]
  transfers between devices with their start and end apart: 1 -> 3, of which waited for: 1 -> 0; matrix products, arithmetic and copies ran while one was open for 0% -> 0% of each run, Pallas kernels for 3% -> 6%
where the time goes in v3:
time: 41.6 us; the launch traced here: 41.3 us
  blocking collectives  30.1 us (72%)
  Pallas kernels  6.16 us (15%)
  starting transfers between devices  5.04 us (12%)
    all_to_all x1, blocking collectives, body(): lax.all_to_all(blocks, 'dom', split_axis=0, concat_axis=0, tiled=True)  19.2 us
    all_to_all x1, blocking collectives, body(): lax.all_to_all(incoming, 'dom', split_axis=0, concat_axis=0, tiled=True)  10.8 us
    ppermute x3, starting transfers between devices, body(): lax.ppermute(panel_signal, 'tm', [(p, (p + back) % N_TM) for p in range(N...  5.04 us
    pallas_call x1, Pallas kernels, body(): pl.pallas_call(tables_kernel, out_shape=(jax.ShapeDtypeStruct((BOXES * J,...  2.63 us
    pallas_call x1, Pallas kernels, body(): pl.pallas_call(translate_kernel, out_shape=jax.ShapeDtypeStruct((N_DOM, 8...  1.58 us
    pallas_call x1, Pallas kernels, body(): pl.pallas_call(receive_kernel, out_shape=jax.ShapeDtypeStruct((2, PAN_DEV...  1.35 us
  transfers between devices with their start and end apart: 3, of which 0 were waited for; matrix products, arithmetic and copies ran while one was open for 0% of the time, Pallas kernels for 6%

profile of v3, /device:TPU:1, one launch (start us, length us, event | category | flops | bytes accessed | tf_op | source)
XLA Modules:
  0.0 41.3 jit_solution(13345563111204645012)
XLA Ops:
  0.0 2.0 %collective-permute-start = (bf16[2,1024]{1,0:T(2,128)(2,1)}, bf16[2,1024]{1,0:T(2,128)(2,1)S(1)}, u32[]{:S(2)}, u32[]{:S(2)}) collective-permute-start(bf16[2,1024]{1,0:T(2,128)(2,1)} %signal_hbm.1), channel_id=1, source_target_pairs={{0,1},{1,2},{2,3},{3,0},{4,5},{5,6},{6,7},{7,4},{8,9},{9,10},{10,1... | collective-permute-start | bytes 12296 | tf_op jit(solution)/shard_map/ppermute | solution.py:196
  2.0 1.3 %collective-permute-start.2 = (bf16[2,1024]{1,0:T(2,128)(2,1)}, bf16[2,1024]{1,0:T(2,128)(2,1)S(1)}, u32[]{:S(2)}, u32[]{:S(2)}) collective-permute-start(bf16[2,1024]{1,0:T(2,128)(2,1)} %signal_hbm.1), channel_id=1, source_target_pairs={{0,3},{1,0},{2,1},{3,2},{4,7},{5,4},{6,5},{7,6},{8,11},{9,8},{10,9... | collective-permute-start | bytes 12296 | tf_op jit(solution)/shard_map/ppermute | solution.py:196
  3.3 1.7 %collective-permute-start.1 = (bf16[2,1024]{1,0:T(2,128)(2,1)}, bf16[2,1024]{1,0:T(2,128)(2,1)S(1)}, u32[]{:S(2)}, u32[]{:S(2)}) collective-permute-start(bf16[2,1024]{1,0:T(2,128)(2,1)} %signal_hbm.1), channel_id=1, source_target_pairs={{0,2},{1,3},{2,0},{3,1},{4,6},{5,7},{6,4},{7,5},{8,10},{9,11},{10,... | collective-permute-start | bytes 12296 | tf_op jit(solution)/shard_map/ppermute | solution.py:196
  5.0 2.6 %tables.1 = (bf16[4096,512]{1,0:T(8,128)(2,1)S(1)}, f32[4096,512]{1,0:T(8,128)S(1)}, bf16[2,1024]{1,0:T(2,128)(2,1)S(1)}, s32[1,1024]{1,0:T(1,128)S(1)}, bf16[1024,1024]{1,0:T(8,128)(2,1)S(1)}) custom-call(s32[8,512]{1,0:T(8,128)} %bitcast.10, s32[8,512]{1,0:T(8,128)} %bitcast.11, s32[1,512]{1,0:T(1,128)} %bitcast.13, bf16[256,64]{1,0:T(8,128)(2,1)} %bitcast.9, ...), custom_call_target="tpu_custom_call" | custom-call | flops 268435456 | bytes 12582912 | tf_op jit(solution)/shard_map/tables/pallas_call | solution.py:199
  7.7 0.0 collective-permute-done.one_ref
  7.7 0.0 collective-permute-done.2.three_ref
  7.7 0.0 collective-permute-done.1.two_ref
  7.7 0.6 %aggregate.1 = bf16[128,8,128]{2,1,0:T(8,128)(2,1)S(1)} custom-call(bf16[2,1024]{1,0:T(2,128)(2,1)S(1)} %get-tuple-element.10.own_ref, bf16[2,1024]{1,0:T(2,128)(2,1)S(1)} %collective-permute-done.one_ref, bf16[2,1024]{1,0:T(2,128)(2,1)S(1)} %collective-permute-done.1.two_ref, bf16[2,1024]{1,0:T(2,128)(2,1)S(1)} %collective-permute-done.2.three_ref, ...), custom_call_target="tpu_custom_call" | custom-call | tf_op jit(solution)/shard_map/aggregate/pallas_call | solution.py:231
  8.3 19.2 %all_to_all.10 = bf16[128,8,128]{2,1,0:T(8,128)(2,1)S(1)} all-to-all(bf16[128,8,128]{2,1,0:T(8,128)(2,1)S(1)} %aggregate.1), channel_id=1, replica_groups=mesh['dom'=32,'tm'=4] {'dom'}, dimensions={0} | all-to-all | bytes 524288 | tf_op jit(solution)/shard_map/all_to_all | solution.py:239
  27.6 0.0 copy-start
  27.6 1.6 %translate.1 = bf16[32,8,128]{2,1,0:T(8,128)(2,1)S(1)} custom-call(bf16[32,4,8,128]{3,2,1,0:T(8,128)(2,1)S(1)} %bitcast.8, bf16[4096,512]{1,0:T(8,128)(2,1)S(1)} %get-tuple-element.13.pick_ref, f32[4096,512]{1,0:T(8,128)S(1)} %get-tuple-element.14.weight_ref), custom_call_target="tpu_custom_call" | custom-call | tf_op jit(solution)/shard_map/translate/pallas_call | solution.py:241
  29.1 10.8 %all_to_all.11.rays_ref = bf16[32,8,128]{2,1,0:T(8,128)(2,1)S(1)} all-to-all(bf16[32,8,128]{2,1,0:T(8,128)(2,1)S(1)} %translate.1), channel_id=1, replica_groups=mesh['dom'=32,'tm'=4] {'dom'}, dimensions={0} | all-to-all | bytes 131072 | tf_op jit(solution)/shard_map/all_to_all | solution.py:255
  40.0 0.0 copy-done
  40.0 1.4 %receive.1 = bf16[2,1024]{1,0:T(2,128)(2,1)} custom-call(bf16[32,8,128]{2,1,0:T(8,128)(2,1)S(1)} %all_to_all.11.rays_ref, s32[1,1024]{1,0:T(1,128)S(1)} %get-tuple-element.11.box_ref, bf16[1024,1024]{1,0:T(8,128)(2,1)S(1)} %copy-done), custom_call_target="tpu_custom_call" | custom-call | tf_op jit(solution)/shard_map/receive/pallas_call | solution.py:256
Async XLA Ops:
  0.0 7.7 %collective-permute-start = (bf16[2,1024]{1,0:T(2,128)(2,1)}, bf16[2,1024]{1,0:T(2,128)(2,1)S(1)}, u32[]{:S(2)}, u32[]{:S(2)}) collective-permute-start(bf16[2,1024]{1,0:T(2,128)(2,1)} %signal_hbm.1), channel_id=1, source_target_pairs={{0,1},{1,2},{2,3},{3,0},{4,5},{5,6},{6,7},{7,4},{8,9},{9,10},{10,1... | collective-permute-start | bytes 12296 | tf_op jit(solution)/shard_map/ppermute | solution.py:196
  2.0 5.7 %collective-permute-start.2 = (bf16[2,1024]{1,0:T(2,128)(2,1)}, bf16[2,1024]{1,0:T(2,128)(2,1)S(1)}, u32[]{:S(2)}, u32[]{:S(2)}) collective-permute-start(bf16[2,1024]{1,0:T(2,128)(2,1)} %signal_hbm.1), channel_id=1, source_target_pairs={{0,3},{1,0},{2,1},{3,2},{4,7},{5,4},{6,5},{7,6},{8,11},{9,8},{10,9... | collective-permute-start | bytes 12296 | tf_op jit(solution)/shard_map/ppermute | solution.py:196
  3.3 4.4 %collective-permute-start.1 = (bf16[2,1024]{1,0:T(2,128)(2,1)}, bf16[2,1024]{1,0:T(2,128)(2,1)S(1)}, u32[]{:S(2)}, u32[]{:S(2)}) collective-permute-start(bf16[2,1024]{1,0:T(2,128)(2,1)} %signal_hbm.1), channel_id=1, source_target_pairs={{0,2},{1,3},{2,0},{3,1},{4,6},{5,7},{6,4},{7,5},{8,10},{9,11},{10,... | collective-permute-start | bytes 12296 | tf_op jit(solution)/shard_map/ppermute | solution.py:196
  27.6 12.4 %copy-start = (bf16[1024,1024]{1,0:T(8,128)(2,1)S(1)}, bf16[1024,1024]{1,0:T(8,128)(2,1)}, u32[]{:S(2)}) copy-start(bf16[1024,1024]{1,0:T(8,128)(2,1)} %reception_ref.1) | copy-start | bytes 6291460

commit v4 on v2

--- a/solution.py
+++ b/solution.py
@@ -33,14 +33,15 @@
 
 
 def aggregate_kernel(
-    signal_hbm, box_hbm, radiation_hbm, source_hbm, class_hbm, count_hbm,
-    out_ref, pick_ref, hot_ref,
-    signal_ref, box_ref, radiation_ref, source_ref, class_ref, count_ref, sems,
+    signal_hbm, box_hbm, radiation_hbm, source_hbm, class_hbm, count_hbm, table_hbm,
+    out_ref, pick_ref, weight_ref, box_ref,
+    signal_ref, radiation_ref, source_ref, class_ref, count_ref, table_ref, rhs_ref, sems,
 ):
     small = [
         (source_hbm, source_ref),
         (class_hbm, class_ref),
         (count_hbm, count_ref),
+        (table_hbm, table_ref),
         (signal_hbm, signal_ref),
         (box_hbm, box_ref),
     ]
@@ -56,23 +57,39 @@
     for copy in copies:
         copy.start()
 
-    for copy in copies[:3]:
+    for copy in copies[:4]:
         copy.wait()
+    first = lax.axis_index("tm") * 2
+    for step_out in range(2):
+        for step_in in range(LAGS):
+            lag = first + step_out - step_in
+            start = pl.multiple_of(jnp.maximum(lag, 0) * DIRS, DIRS)
+            rows = table_ref[pl.ds(start, DIRS), :]
+            rows = jnp.where(lag >= 0, rows, jnp.zeros_like(rows))
+            rhs_ref[pl.ds((step_out * LAGS + step_in) * DIRS, DIRS), :] = rows
+    rhs = rhs_ref[...]
     used = lax.broadcasted_iota(jnp.int32, (J, BOXES), 0) < count_ref[...]
     classes = jnp.transpose(jnp.where(used, class_ref[...], -1))
     sources = jnp.transpose(source_ref[...])
     lane_s = lax.broadcasted_iota(jnp.int32, (CHUNK, BOXES), 1)
     lane_c = lax.broadcasted_iota(jnp.int32, (CHUNK, CLASSES), 1)
     for chunk in range(N_CHUNK):
+        hots = []
         for j in range(J):
             rows = slice(chunk * CHUNK, chunk * CHUNK + CHUNK)
             at = pl.ds((chunk * J + j) * CHUNK, CHUNK)
             src = sources[rows, j : j + 1]
             cls = classes[rows, j : j + 1]
             pick_ref[at, :] = (src == lane_s).astype(jnp.float32).astype(jnp.bfloat16)
-            hot_ref[at, :] = (cls == lane_c).astype(jnp.float32).astype(jnp.bfloat16)
-
-    for copy in copies[3:5]:
+            hots.append((cls == lane_c).astype(jnp.float32).astype(jnp.bfloat16))
+        weight_ref[pl.ds(chunk * J * CHUNK, J * CHUNK), :] = lax.dot_general(
+            jnp.concatenate(hots, axis=0),
+            rhs,
+            (((1,), (1,)), ((), ())),
+            preferred_element_type=jnp.float32,
+        )
+
+    for copy in copies[4:6]:
         copy.wait()
     signal = signal_ref[...].astype(jnp.float32)
     parts = []
@@ -83,7 +100,7 @@
     masked = jnp.concatenate(parts, axis=0).astype(jnp.bfloat16)
     rays = jnp.zeros((32, K), jnp.float32)
     for part in range(N_LOAD):
-        copies[5 + part].wait()
+        copies[6 + part].wait()
         rows = slice(part * height, part * height + height)
         rays = rays + jnp.dot(
             masked[:, rows], radiation_ref[rows, :], preferred_element_type=jnp.float32
@@ -102,17 +119,7 @@
                 out_ref[(column * 4 + g) * N_TM + plane] = tile
 
 
-def translate_kernel(
-    rays_ref, pick_ref, hot_ref, table_ref, out_ref, near_ref, rhs_ref, weight_ref, got_ref, sum_ref
-):
-    first = lax.axis_index("tm") * 2
-    for step_out in range(2):
-        for step_in in range(LAGS):
-            lag = first + step_out - step_in
-            start = pl.multiple_of(jnp.maximum(lag, 0) * DIRS, DIRS)
-            rows = table_ref[pl.ds(start, DIRS), :]
-            rows = jnp.where(lag >= 0, rows, jnp.zeros_like(rows))
-            rhs_ref[pl.ds((step_out * LAGS + step_in) * DIRS, DIRS), :] = rows
+def translate_kernel(rays_ref, pick_ref, weight_ref, out_ref, near_ref, got_ref, sum_ref):
     low = lax.broadcasted_iota(jnp.int32, (N_DOM, 8, 128), 2) < 64
     for pair in range(2):
         left = rays_ref[:, 2 * pair].astype(jnp.float32)
@@ -125,12 +132,6 @@
     for chunk in range(N_CHUNK):
         base = chunk * rows_chunk
         rows = slice(base, base + rows_chunk)
-        weight_ref[rows, :] = lax.dot_general(
-            hot_ref[rows, :],
-            rhs_ref[...],
-            (((1,), (1,)), ((), ())),
-            preferred_element_type=jnp.float32,
-        )
         got_ref[rows, :] = jnp.dot(
             pick_ref[rows, :], near_ref[...], preferred_element_type=jnp.float32
         )
@@ -202,23 +203,25 @@
     panel_signal, panel_box, radiation, reception, translation, list_source, list_class, list_count
 ):
     boxes_row = panel_box.reshape(1, PAN_DEV)
-    blocks, pick, hot = pl.pallas_call(
+    blocks, pick, weight, own_box = pl.pallas_call(
         aggregate_kernel,
         out_shape=(
             jax.ShapeDtypeStruct((N_DOM * N_TM, 8, 128), jnp.bfloat16),
             jax.ShapeDtypeStruct((BOXES * J, BOXES), jnp.bfloat16),
-            jax.ShapeDtypeStruct((BOXES * J, CLASSES), jnp.bfloat16),
+            jax.ShapeDtypeStruct((BOXES * J, 2 * LAGS * DIRS), jnp.float32),
+            jax.ShapeDtypeStruct((1, PAN_DEV), jnp.int32),
         ),
-        in_specs=[HBM] * 6,
-        out_specs=(VMEM,) * 3,
+        in_specs=[HBM] * 7,
+        out_specs=(VMEM,) * 4,
         scratch_shapes=[
             pltpu.VMEM((2, PAN_DEV), jnp.bfloat16),
-            pltpu.VMEM((1, PAN_DEV), jnp.int32),
             pltpu.VMEM((PAN_DEV, K), jnp.bfloat16),
             pltpu.VMEM((J, BOXES), jnp.int32),
             pltpu.VMEM((J, BOXES), jnp.int32),
             pltpu.VMEM((1, BOXES), jnp.int32),
-            pltpu.SemaphoreType.DMA((5 + N_LOAD,)),
+            pltpu.VMEM((LAGS * DIRS, CLASSES), jnp.bfloat16),
+            pltpu.VMEM((2 * LAGS * DIRS, CLASSES), jnp.bfloat16),
+            pltpu.SemaphoreType.DMA((6 + N_LOAD,)),
         ],
         compiler_params=params(40),
         name="aggregate",
@@ -229,29 +232,23 @@
         in_hbm(list_source.T),
         in_hbm(list_class.T),
         in_hbm(list_count.reshape(1, BOXES)),
+        in_hbm(jnp.transpose(translation, (1, 2, 0)).reshape(LAGS * DIRS, CLASSES)),
     )
     spread = lax.all_to_all(blocks, ("dom", "tm"), split_axis=0, concat_axis=0, tiled=True)
 
     incoming = pl.pallas_call(
         translate_kernel,
         out_shape=jax.ShapeDtypeStruct((N_DOM, 8, 128), jnp.bfloat16),
-        in_specs=[VMEM] * 4,
+        in_specs=[VMEM] * 3,
         out_specs=VMEM,
         scratch_shapes=[
             pltpu.VMEM((BOXES, 256), jnp.bfloat16),
-            pltpu.VMEM((2 * LAGS * DIRS, CLASSES), jnp.bfloat16),
-            pltpu.VMEM((BOXES * J, 512), jnp.float32),
             pltpu.VMEM((BOXES * J, 256), jnp.float32),
             pltpu.VMEM((BOXES, 256), jnp.float32),
         ],
-        compiler_params=params(40),
+        compiler_params=params(32),
         name="translate",
-    )(
-        spread.reshape(N_DOM, N_TM, 8, 128),
-        pick,
-        hot,
-        jnp.transpose(translation, (1, 2, 0)).reshape(LAGS * DIRS, CLASSES),
-    )
+    )(spread.reshape(N_DOM, N_TM, 8, 128), pick, weight)
 
     rays = lax.all_to_all(incoming, "dom", split_axis=0, concat_axis=0, tiled=True)
     return pl.pallas_call(
@@ -261,7 +258,7 @@
         out_specs=VMEM,
         compiler_params=params(16),
         name="receive",
-    )(rays, boxes_row, reception)
+    )(rays, own_box, reception)
 
 
 def solution(mesh):

time: 40.9 us -> 40.5 us (level)
  Pallas kernels: 6.88 us -> 6.43 us
    pallas_call x1, Pallas kernels: 2.59 us -> 1.78 us  [body(): pl.pallas_call(translate_kernel, out_shape=jax.ShapeDtypeStruct((N_DOM, 8...]
where the time goes in v4:
time: 40.5 us; the launch traced here: 40.3 us
  blocking collectives  33.8 us (83%)
  Pallas kernels  6.43 us (16%)
    all_to_all x1, blocking collectives, body(): lax.all_to_all(blocks, ('dom', 'tm'), split_axis=0, concat_axis=0, tiled=...  22.6 us
    all_to_all x1, blocking collectives, body(): lax.all_to_all(incoming, 'dom', split_axis=0, concat_axis=0, tiled=True)  11.2 us
    pallas_call x1, Pallas kernels, body(): pl.pallas_call(aggregate_kernel, out_shape=(jax.ShapeDtypeStruct((N_DOM *...  3.29 us
    pallas_call x1, Pallas kernels, body(): pl.pallas_call(translate_kernel, out_shape=jax.ShapeDtypeStruct((N_DOM, 8...  1.78 us
    pallas_call x1, Pallas kernels, body(): pl.pallas_call(receive_kernel, out_shape=jax.ShapeDtypeStruct((2, PAN_DEV...  1.36 us

profile of v4, /device:TPU:1, one launch (start us, length us, event | category | flops | bytes accessed | tf_op | source)
XLA Modules:
  0.0 40.3 jit_solution(3141242837115144872)
XLA Ops:
  0.0 3.3 %aggregate.1 = (bf16[128,8,128]{2,1,0:T(8,128)(2,1)S(1)}, bf16[4096,512]{1,0:T(8,128)(2,1)S(1)}, f32[4096,512]{1,0:T(8,128)S(1)}, s32[1,1024]{1,0:T(1,128)S(1)}) custom-call(bf16[2,1024]{1,0:T(2,128)(2,1)} %signal_hbm.1, s32[1,1024]{1,0:T(1,128)} %bitcast.12, bf16[1024,1024]{1,0:T(8,128)(2,1)} %radiation_hbm.1, s32[8,512]{1,0:T(8,128)} %bitcast.10, ...), custom_call_target="tpu_custom_call" | custom-call | tf_op jit(solution)/shard_map/aggregate/pallas_call | solution.py:206
  3.3 22.6 %all_to_all.10 = bf16[128,8,128]{2,1,0:T(8,128)(2,1)S(1)} all-to-all(bf16[128,8,128]{2,1,0:T(8,128)(2,1)S(1)} %get-tuple-element.9), channel_id=1, replica_groups=mesh['dom'=32,'tm'=4] {'dom','tm'}, dimensions={0} | all-to-all | bytes 524288 | tf_op jit(solution)/shard_map/all_to_all | solution.py:237
  25.9 0.0 copy-start
  25.9 1.8 %translate.1 = bf16[32,8,128]{2,1,0:T(8,128)(2,1)S(1)} custom-call(bf16[32,4,8,128]{3,2,1,0:T(8,128)(2,1)S(1)} %bitcast.8, bf16[4096,512]{1,0:T(8,128)(2,1)S(1)} %get-tuple-element.10.pick_ref, f32[4096,512]{1,0:T(8,128)S(1)} %get-tuple-element.11.weight_ref), custom_call_target="tpu_custom_call" | custom-call | tf_op jit(solution)/shard_map/translate/pallas_call | solution.py:239
  27.7 11.2 %all_to_all.11.rays_ref = bf16[32,8,128]{2,1,0:T(8,128)(2,1)S(1)} all-to-all(bf16[32,8,128]{2,1,0:T(8,128)(2,1)S(1)} %translate.1), channel_id=1, replica_groups=mesh['dom'=32,'tm'=4] {'dom'}, dimensions={0} | all-to-all | bytes 131072 | tf_op jit(solution)/shard_map/all_to_all | solution.py:253
  38.9 0.0 copy-done
  38.9 1.4 %receive.1 = bf16[2,1024]{1,0:T(2,128)(2,1)} custom-call(bf16[32,8,128]{2,1,0:T(8,128)(2,1)S(1)} %all_to_all.11.rays_ref, s32[1,1024]{1,0:T(1,128)S(1)} %get-tuple-element.12.box_ref, bf16[1024,1024]{1,0:T(8,128)(2,1)S(1)} %copy-done), custom_call_target="tpu_custom_call" | custom-call | tf_op jit(solution)/shard_map/receive/pallas_call | solution.py:254
Async XLA Ops:
  25.9 13.0 %copy-start = (bf16[1024,1024]{1,0:T(8,128)(2,1)S(1)}, bf16[1024,1024]{1,0:T(8,128)(2,1)}, u32[]{:S(2)}) copy-start(bf16[1024,1024]{1,0:T(8,128)(2,1)} %reception_ref.1) | copy-start | bytes 6291460

commit v5 on v4

--- a/solution.py
+++ b/solution.py
@@ -16,9 +16,8 @@
 PAN_DEV = 1024
 K = 1024
 GROUPS = K // 128
-CHUNK = 128
-N_CHUNK = BOXES // CHUNK
-N_LOAD = 4
+N_CHUNK = BOXES // 128
+N_LOAD = 8
 VMEM = pl.BlockSpec(memory_space=pltpu.VMEM)
 HBM = pl.BlockSpec(memory_space=pltpu.HBM)
 
@@ -35,7 +34,7 @@
 def aggregate_kernel(
     signal_hbm, box_hbm, radiation_hbm, source_hbm, class_hbm, count_hbm, table_hbm,
     out_ref, pick_ref, weight_ref, box_ref,
-    signal_ref, radiation_ref, source_ref, class_ref, count_ref, table_ref, rhs_ref, sems,
+    signal_ref, radiation_ref, source_ref, class_ref, count_ref, table_ref, sems,
 ):
     small = [
         (source_hbm, source_ref),
@@ -57,37 +56,45 @@
     for copy in copies:
         copy.start()
 
+    row = lax.broadcasted_iota(jnp.int32, (16, 128), 0)
+    pattern = row // 8 * BOX_DEV + row % 8
+    kind = lax.broadcasted_iota(jnp.int32, (CLASSES, 128), 0)
+    one, zero = jnp.bfloat16(1), jnp.bfloat16(0)
     for copy in copies[:4]:
         copy.wait()
     first = lax.axis_index("tm") * 2
-    for step_out in range(2):
-        for step_in in range(LAGS):
-            lag = first + step_out - step_in
-            start = pl.multiple_of(jnp.maximum(lag, 0) * DIRS, DIRS)
-            rows = table_ref[pl.ds(start, DIRS), :]
-            rows = jnp.where(lag >= 0, rows, jnp.zeros_like(rows))
-            rhs_ref[pl.ds((step_out * LAGS + step_in) * DIRS, DIRS), :] = rows
-    rhs = rhs_ref[...]
+    parts = []
+    for step in range(LAGS):
+        lag = first + 1 - step
+        start = pl.multiple_of(jnp.maximum(lag, 0) * DIRS, DIRS)
+        rows = table_ref[pl.ds(start, DIRS), :]
+        parts.append(jnp.where(lag >= 0, rows, jnp.zeros_like(rows)))
+    lagged = jnp.concatenate(parts, axis=0)
     used = lax.broadcasted_iota(jnp.int32, (J, BOXES), 0) < count_ref[...]
-    classes = jnp.transpose(jnp.where(used, class_ref[...], -1))
-    sources = jnp.transpose(source_ref[...])
-    lane_s = lax.broadcasted_iota(jnp.int32, (CHUNK, BOXES), 1)
-    lane_c = lax.broadcasted_iota(jnp.int32, (CHUNK, CLASSES), 1)
+    classes = jnp.where(used, class_ref[...], -1)
+    sources = source_ref[...]
+    wide = [
+        jnp.broadcast_to(sources[j : j + 1, at : at + 128], (16, 128)).astype(jnp.int16)
+        for at in range(0, BOXES, 128)
+        for j in range(J)
+    ]
     for chunk in range(N_CHUNK):
-        hots = []
-        for j in range(J):
-            rows = slice(chunk * CHUNK, chunk * CHUNK + CHUNK)
-            at = pl.ds((chunk * J + j) * CHUNK, CHUNK)
-            src = sources[rows, j : j + 1]
-            cls = classes[rows, j : j + 1]
-            pick_ref[at, :] = (src == lane_s).astype(jnp.float32).astype(jnp.bfloat16)
-            hots.append((cls == lane_c).astype(jnp.float32).astype(jnp.bfloat16))
-        weight_ref[pl.ds(chunk * J * CHUNK, J * CHUNK), :] = lax.dot_general(
-            jnp.concatenate(hots, axis=0),
-            rhs,
-            (((1,), (1,)), ((), ())),
-            preferred_element_type=jnp.float32,
-        )
+        lanes = slice(chunk * 128, chunk * 128 + 128)
+        hots = [
+            (classes[j : j + 1, lanes] == kind).astype(jnp.float32).astype(jnp.bfloat16)
+            for j in range(J)
+        ]
+        at = slice(chunk * J * 128, (chunk + 1) * J * 128)
+        weight_ref[:, at] = jnp.dot(
+            lagged, jnp.concatenate(hots, axis=1), preferred_element_type=jnp.float32
+        )
+        for low in range(chunk * 128, chunk * 128 + 128, 16):
+            box = low % 256 // 8 * BOX_DEV + low // 256 * 8
+            here = (pattern + box).astype(jnp.int16)
+            for index, source in enumerate(wide):
+                pick_ref[low : low + 16, index * 128 : index * 128 + 128] = jnp.where(
+                    source == here, one, zero
+                )
 
     for copy in copies[4:6]:
         copy.wait()
@@ -120,46 +127,46 @@
 
 
 def translate_kernel(rays_ref, pick_ref, weight_ref, out_ref, near_ref, got_ref, sum_ref):
-    low = lax.broadcasted_iota(jnp.int32, (N_DOM, 8, 128), 2) < 64
-    for pair in range(2):
-        left = rays_ref[:, 2 * pair].astype(jnp.float32)
-        right = rays_ref[:, 2 * pair + 1].astype(jnp.float32)
-        upper = jnp.where(low, left, pltpu.roll(right, 64, 2))
-        lower = jnp.where(low, pltpu.roll(left, 64, 2), right)
-        both = jnp.concatenate([upper[:, None], lower[:, None]], axis=1)
-        near_ref[:, pair * 128 : pair * 128 + 128] = both.reshape(BOXES, 128).astype(jnp.bfloat16)
-    rows_chunk = J * CHUNK
+    for plane in range(N_TM):
+        turned = jnp.transpose(rays_ref[:, plane].astype(jnp.float32).reshape(256, 128))
+        turned = turned.astype(jnp.bfloat16)
+        for half in range(2):
+            near_ref[plane * 64 : plane * 64 + 64, half * 256 : half * 256 + 256] = turned[
+                half * 64 : half * 64 + 64
+            ]
     for chunk in range(N_CHUNK):
-        base = chunk * rows_chunk
-        rows = slice(base, base + rows_chunk)
-        got_ref[rows, :] = jnp.dot(
-            pick_ref[rows, :], near_ref[...], preferred_element_type=jnp.float32
-        )
-        for piece in range(CHUNK // 16):
-            total = [jnp.zeros((16, 128), jnp.float32) for _ in range(2)]
+        at = slice(chunk * J * 128, (chunk + 1) * J * 128)
+        got_ref[:, at] = jnp.dot(
+            near_ref[...], pick_ref[:, at], preferred_element_type=jnp.float32
+        )
+        for low in range(0, DIRS, 8):
+            total = [jnp.zeros((8, 128), jnp.float32) for _ in range(2)]
             for j in range(J):
-                at = base + j * CHUNK + piece * 16
-                for side in range(2):
-                    got = got_ref[at : at + 16, side * 128 : side * 128 + 128]
-                    for step in range(2):
-                        lanes = slice(step * 256 + side * 128, step * 256 + side * 128 + 128)
-                        total[step] = total[step] + weight_ref[at : at + 16, lanes] * got
+                lanes = slice((chunk * J + j) * 128, (chunk * J + j) * 128 + 128)
+                for step in range(LAGS):
+                    weight = weight_ref[step * DIRS + low : step * DIRS + low + 8, lanes]
+                    at_step = step * DIRS + low
+                    total[1] = total[1] + weight * got_ref[at_step : at_step + 8, lanes]
+                    if step > 0:
+                        at_step = at_step - DIRS
+                        total[0] = total[0] + weight * got_ref[at_step : at_step + 8, lanes]
             for step in range(2):
-                at = chunk * CHUNK + piece * 16
-                sum_ref[at : at + 16, step * 128 : step * 128 + 128] = total[step]
-    even = lane_group((N_DOM, 8, 128)) % 2 == 0
-    merged = []
-    for half in range(2):
-        one = sum_ref[:, 0:128].reshape(N_DOM, 2, 8, 128)[:, half]
-        two = sum_ref[:, 128:256].reshape(N_DOM, 2, 8, 128)[:, half]
-        merged.append(
-            jnp.where(even, one, two)
-            + jnp.where(even, pltpu.roll(one, 96, 2), pltpu.roll(two, 32, 2))
-        )
-    final = jnp.where(low, merged[0], merged[1]) + pltpu.roll(
-        jnp.where(low, merged[1], merged[0]), 64, 2
-    )
-    out_ref[...] = final.astype(jnp.bfloat16)
+                at_row = chunk % 2 * 64 + step * DIRS + low
+                sum_ref[at_row : at_row + 8, chunk // 2 * 128 : chunk // 2 * 128 + 128] = total[
+                    step
+                ]
+        if chunk % 2 == 1:
+            pair = jnp.transpose(sum_ref[:, chunk // 2 * 128 : chunk // 2 * 128 + 128])
+            pair = pair.reshape(8, 2, 8, 128)
+            upper, lower = pair[:, 0], pair[:, 1]
+            left = lax.broadcasted_iota(jnp.int32, (8, 8, 128), 2) < 64
+            tiles = (
+                jnp.where(left, upper, pltpu.roll(lower, 64, 2)),
+                jnp.where(left, pltpu.roll(upper, 64, 2), lower),
+            )
+            for side in range(2):
+                at_box = (chunk - 1 + side) * 8
+                out_ref[at_box : at_box + 8] = tiles[side].astype(jnp.bfloat16)
 
 
 def receive_kernel(rays_ref, box_ref, reception_ref, out_ref):
@@ -207,8 +214,8 @@
         aggregate_kernel,
         out_shape=(
             jax.ShapeDtypeStruct((N_DOM * N_TM, 8, 128), jnp.bfloat16),
-            jax.ShapeDtypeStruct((BOXES * J, BOXES), jnp.bfloat16),
-            jax.ShapeDtypeStruct((BOXES * J, 2 * LAGS * DIRS), jnp.float32),
+            jax.ShapeDtypeStruct((BOXES, BOXES * J), jnp.bfloat16),
+            jax.ShapeDtypeStruct((LAGS * DIRS, BOXES * J), jnp.float32),
             jax.ShapeDtypeStruct((1, PAN_DEV), jnp.int32),
         ),
         in_specs=[HBM] * 7,
@@ -220,7 +227,6 @@
             pltpu.VMEM((J, BOXES), jnp.int32),
             pltpu.VMEM((1, BOXES), jnp.int32),
             pltpu.VMEM((LAGS * DIRS, CLASSES), jnp.bfloat16),
-            pltpu.VMEM((2 * LAGS * DIRS, CLASSES), jnp.bfloat16),
             pltpu.SemaphoreType.DMA((6 + N_LOAD,)),
         ],
         compiler_params=params(40),
@@ -242,9 +248,9 @@
         in_specs=[VMEM] * 3,
         out_specs=VMEM,
         scratch_shapes=[
-            pltpu.VMEM((BOXES, 256), jnp.bfloat16),
-            pltpu.VMEM((BOXES * J, 256), jnp.float32),
-            pltpu.VMEM((BOXES, 256), jnp.float32),
+            pltpu.VMEM((LAGS * DIRS, BOXES), jnp.bfloat16),
+            pltpu.VMEM((LAGS * DIRS, BOXES * J), jnp.float32),
+            pltpu.VMEM((128, BOXES // 2), jnp.float32),
         ],
         compiler_params=params(32),
         name="translate",

time: 40.5 us -> 40 us (0.988)
  Pallas kernels: 6.43 us -> 6 us
    pallas_call x1, Pallas kernels: 3.29 us -> 2.86 us  [body(): pl.pallas_call(aggregate_kernel, out_shape=(jax.ShapeDtypeStruct((N_DOM *...]
where the time goes in v5:
time: 40 us; the launch traced here: 39.9 us
  blocking collectives  33.8 us (84%)
  Pallas kernels  6 us (15%)
    all_to_all x1, blocking collectives, body(): lax.all_to_all(blocks, ('dom', 'tm'), split_axis=0, concat_axis=0, tiled=...  22.6 us
    all_to_all x1, blocking collectives, body(): lax.all_to_all(incoming, 'dom', split_axis=0, concat_axis=0, tiled=True)  11.2 us
    pallas_call x1, Pallas kernels, body(): pl.pallas_call(aggregate_kernel, out_shape=(jax.ShapeDtypeStruct((N_DOM *...  2.86 us
    pallas_call x1, Pallas kernels, body(): pl.pallas_call(translate_kernel, out_shape=jax.ShapeDtypeStruct((N_DOM, 8...  1.78 us
    pallas_call x1, Pallas kernels, body(): pl.pallas_call(receive_kernel, out_shape=jax.ShapeDtypeStruct((2, PAN_DEV...  1.36 us

profile of v5, /device:TPU:1, one launch (start us, length us, event | category | flops | bytes accessed | tf_op | source)
XLA Modules:
  0.0 39.9 jit_solution(7251773927086542251)
XLA Ops:
  0.0 2.9 %aggregate.1 = (bf16[128,8,128]{2,1,0:T(8,128)(2,1)S(1)}, bf16[512,4096]{1,0:T(8,128)(2,1)S(1)}, f32[256,4096]{1,0:T(8,128)S(1)}, s32[1,1024]{1,0:T(1,128)S(1)}) custom-call(bf16[2,1024]{1,0:T(2,128)(2,1)} %signal_hbm.1, s32[1,1024]{1,0:T(1,128)} %bitcast.12, bf16[1024,1024]{1,0:T(8,128)(2,1)} %radiation_hbm.1, s32[8,512]{1,0:T(8,128)} %bitcast.10, ...), custom_call_target="tpu_custom_call" | custom-call | tf_op jit(solution)/shard_map/aggregate/pallas_call | solution.py:213
  2.9 22.6 %all_to_all.10 = bf16[128,8,128]{2,1,0:T(8,128)(2,1)S(1)} all-to-all(bf16[128,8,128]{2,1,0:T(8,128)(2,1)S(1)} %get-tuple-element.9), channel_id=1, replica_groups=mesh['dom'=32,'tm'=4] {'dom','tm'}, dimensions={0} | all-to-all | bytes 524288 | tf_op jit(solution)/shard_map/all_to_all | solution.py:243
  25.5 0.0 copy-start
  25.5 1.8 %translate.1 = bf16[32,8,128]{2,1,0:T(8,128)(2,1)S(1)} custom-call(bf16[32,4,8,128]{3,2,1,0:T(8,128)(2,1)S(1)} %bitcast.8, bf16[512,4096]{1,0:T(8,128)(2,1)S(1)} %get-tuple-element.10.pick_ref, f32[256,4096]{1,0:T(8,128)S(1)} %get-tuple-element.11.weight_ref), custom_call_target="tpu_custom_call" | custom-call | tf_op jit(solution)/shard_map/translate/pallas_call | solution.py:245
  27.3 11.2 %all_to_all.11.rays_ref = bf16[32,8,128]{2,1,0:T(8,128)(2,1)S(1)} all-to-all(bf16[32,8,128]{2,1,0:T(8,128)(2,1)S(1)} %translate.1), channel_id=1, replica_groups=mesh['dom'=32,'tm'=4] {'dom'}, dimensions={0} | all-to-all | bytes 131072 | tf_op jit(solution)/shard_map/all_to_all | solution.py:259
  38.5 0.0 copy-done
  38.5 1.4 %receive.1 = bf16[2,1024]{1,0:T(2,128)(2,1)} custom-call(bf16[32,8,128]{2,1,0:T(8,128)(2,1)S(1)} %all_to_all.11.rays_ref, s32[1,1024]{1,0:T(1,128)S(1)} %get-tuple-element.12.box_ref, bf16[1024,1024]{1,0:T(8,128)(2,1)S(1)} %copy-done), custom_call_target="tpu_custom_call" | custom-call | tf_op jit(solution)/shard_map/receive/pallas_call | solution.py:260
Async XLA Ops:
  25.5 13.0 %copy-start = (bf16[1024,1024]{1,0:T(8,128)(2,1)S(1)}, bf16[1024,1024]{1,0:T(8,128)(2,1)}, u32[]{:S(2)}) copy-start(bf16[1024,1024]{1,0:T(8,128)(2,1)} %reception_ref.1) | copy-start | bytes 6291460

commit v6 on v5

--- a/solution.py
+++ b/solution.py
@@ -17,7 +17,7 @@
 K = 1024
 GROUPS = K // 128
 N_CHUNK = BOXES // 128
-N_LOAD = 8
+N_LOAD = 1
 VMEM = pl.BlockSpec(memory_space=pltpu.VMEM)
 HBM = pl.BlockSpec(memory_space=pltpu.HBM)
 
@@ -139,22 +139,21 @@
         got_ref[:, at] = jnp.dot(
             near_ref[...], pick_ref[:, at], preferred_element_type=jnp.float32
         )
-        for low in range(0, DIRS, 8):
-            total = [jnp.zeros((8, 128), jnp.float32) for _ in range(2)]
-            for j in range(J):
-                lanes = slice((chunk * J + j) * 128, (chunk * J + j) * 128 + 128)
-                for step in range(LAGS):
-                    weight = weight_ref[step * DIRS + low : step * DIRS + low + 8, lanes]
-                    at_step = step * DIRS + low
-                    total[1] = total[1] + weight * got_ref[at_step : at_step + 8, lanes]
-                    if step > 0:
-                        at_step = at_step - DIRS
-                        total[0] = total[0] + weight * got_ref[at_step : at_step + 8, lanes]
-            for step in range(2):
-                at_row = chunk % 2 * 64 + step * DIRS + low
-                sum_ref[at_row : at_row + 8, chunk // 2 * 128 : chunk // 2 * 128 + 128] = total[
-                    step
-                ]
+        total = [jnp.zeros((DIRS, 128), jnp.float32) for _ in range(2)]
+        for j in range(J):
+            lanes = slice((chunk * J + j) * 128, (chunk * J + j) * 128 + 128)
+            weight, got = weight_ref[0:DIRS, lanes], got_ref[0:DIRS, lanes]
+            even, odd = None, weight * got
+            for step in range(1, LAGS):
+                here = slice(step * DIRS, step * DIRS + DIRS)
+                weight = weight_ref[here, lanes]
+                even = weight * got if even is None else even + weight * got
+                got = got_ref[here, lanes]
+                odd = odd + weight * got
+            total = [total[0] + even, total[1] + odd]
+        for step in range(2):
+            at_row = chunk % 2 * 64 + step * DIRS
+            sum_ref[at_row : at_row + DIRS, chunk // 2 * 128 : chunk // 2 * 128 + 128] = total[step]
         if chunk % 2 == 1:
             pair = jnp.transpose(sum_ref[:, chunk // 2 * 128 : chunk // 2 * 128 + 128])
             pair = pair.reshape(8, 2, 8, 128)

time: 40 us -> 39.8 us (level)
  no operation moved by 1% of the time
where the time goes in v6:
time: 39.8 us; the launch traced here: 39.6 us
  blocking collectives  33.8 us (85%)
  Pallas kernels  5.73 us (14%)
    all_to_all x1, blocking collectives, body(): lax.all_to_all(blocks, ('dom', 'tm'), split_axis=0, concat_axis=0, tiled=...  22.6 us
    all_to_all x1, blocking collectives, body(): lax.all_to_all(incoming, 'dom', split_axis=0, concat_axis=0, tiled=True)  11.2 us
    pallas_call x1, Pallas kernels, body(): pl.pallas_call(aggregate_kernel, out_shape=(jax.ShapeDtypeStruct((N_DOM *...  2.78 us
    pallas_call x1, Pallas kernels, body(): pl.pallas_call(translate_kernel, out_shape=jax.ShapeDtypeStruct((N_DOM, 8...  1.6 us
    pallas_call x1, Pallas kernels, body(): pl.pallas_call(receive_kernel, out_shape=jax.ShapeDtypeStruct((2, PAN_DEV...  1.36 us

profile of v6, /device:TPU:1, one launch (start us, length us, event | category | flops | bytes accessed | tf_op | source)
XLA Modules:
  0.0 39.6 jit_solution(14886957439129371101)
XLA Ops:
  0.0 2.8 %aggregate.1 = (bf16[128,8,128]{2,1,0:T(8,128)(2,1)S(1)}, bf16[512,4096]{1,0:T(8,128)(2,1)S(1)}, f32[256,4096]{1,0:T(8,128)S(1)}, s32[1,1024]{1,0:T(1,128)S(1)}) custom-call(bf16[2,1024]{1,0:T(2,128)(2,1)} %signal_hbm.1, s32[1,1024]{1,0:T(1,128)} %bitcast.12, bf16[1024,1024]{1,0:T(8,128)(2,1)} %radiation_hbm.1, s32[8,512]{1,0:T(8,128)} %bitcast.10, ...), custom_call_target="tpu_custom_call" | custom-call | tf_op jit(solution)/shard_map/aggregate/pallas_call | solution.py:212
  2.8 22.6 %all_to_all.10 = bf16[128,8,128]{2,1,0:T(8,128)(2,1)S(1)} all-to-all(bf16[128,8,128]{2,1,0:T(8,128)(2,1)S(1)} %get-tuple-element.9), channel_id=1, replica_groups=mesh['dom'=32,'tm'=4] {'dom','tm'}, dimensions={0} | all-to-all | bytes 524288 | tf_op jit(solution)/shard_map/all_to_all | solution.py:242
  25.4 0.0 copy-start
  25.4 1.6 %translate.1 = bf16[32,8,128]{2,1,0:T(8,128)(2,1)S(1)} custom-call(bf16[32,4,8,128]{3,2,1,0:T(8,128)(2,1)S(1)} %bitcast.8, bf16[512,4096]{1,0:T(8,128)(2,1)S(1)} %get-tuple-element.10.pick_ref, f32[256,4096]{1,0:T(8,128)S(1)} %get-tuple-element.11.weight_ref), custom_call_target="tpu_custom_call" | custom-call | tf_op jit(solution)/shard_map/translate/pallas_call | solution.py:244
  27.0 11.2 %all_to_all.11.rays_ref = bf16[32,8,128]{2,1,0:T(8,128)(2,1)S(1)} all-to-all(bf16[32,8,128]{2,1,0:T(8,128)(2,1)S(1)} %translate.1), channel_id=1, replica_groups=mesh['dom'=32,'tm'=4] {'dom'}, dimensions={0} | all-to-all | bytes 131072 | tf_op jit(solution)/shard_map/all_to_all | solution.py:258
  38.2 0.0 copy-done
  38.2 1.4 %receive.1 = bf16[2,1024]{1,0:T(2,128)(2,1)} custom-call(bf16[32,8,128]{2,1,0:T(8,128)(2,1)S(1)} %all_to_all.11.rays_ref, s32[1,1024]{1,0:T(1,128)S(1)} %get-tuple-element.12.box_ref, bf16[1024,1024]{1,0:T(8,128)(2,1)S(1)} %copy-done), custom_call_target="tpu_custom_call" | custom-call | tf_op jit(solution)/shard_map/receive/pallas_call | solution.py:259
Async XLA Ops:
  25.4 12.8 %copy-start = (bf16[1024,1024]{1,0:T(8,128)(2,1)S(1)}, bf16[1024,1024]{1,0:T(8,128)(2,1)}, u32[]{:S(2)}) copy-start(bf16[1024,1024]{1,0:T(8,128)(2,1)} %reception_ref.1) | copy-start | bytes 6291460

commit v7 on v6

--- a/solution.py
+++ b/solution.py
@@ -78,6 +78,13 @@
         for at in range(0, BOXES, 128)
         for j in range(J)
     ]
+    for low in range(0, BOXES, 16):
+        box = low % 256 // 8 * BOX_DEV + low // 256 * 8
+        here = (pattern + box).astype(jnp.int16)
+        for index, source in enumerate(wide):
+            pick_ref[low : low + 16, index * 128 : index * 128 + 128] = jnp.where(
+                source == here, one, zero
+            )
     for chunk in range(N_CHUNK):
         lanes = slice(chunk * 128, chunk * 128 + 128)
         hots = [
@@ -88,13 +95,6 @@
         weight_ref[:, at] = jnp.dot(
             lagged, jnp.concatenate(hots, axis=1), preferred_element_type=jnp.float32
         )
-        for low in range(chunk * 128, chunk * 128 + 128, 16):
-            box = low % 256 // 8 * BOX_DEV + low // 256 * 8
-            here = (pattern + box).astype(jnp.int16)
-            for index, source in enumerate(wide):
-                pick_ref[low : low + 16, index * 128 : index * 128 + 128] = jnp.where(
-                    source == here, one, zero
-                )
 
     for copy in copies[4:6]:
         copy.wait()
@@ -128,8 +128,7 @@
 
 def translate_kernel(rays_ref, pick_ref, weight_ref, out_ref, near_ref, got_ref, sum_ref):
     for plane in range(N_TM):
-        turned = jnp.transpose(rays_ref[:, plane].astype(jnp.float32).reshape(256, 128))
-        turned = turned.astype(jnp.bfloat16)
+        turned = jnp.transpose(rays_ref[:, plane].reshape(256, 128))
         for half in range(2):
             near_ref[plane * 64 : plane * 64 + 64, half * 256 : half * 256 + 256] = turned[
                 half * 64 : half * 64 + 64

time: 39.8 us -> 39.8 us (level)
  no operation moved by 1% of the time
where the time goes in v7:
time: 39.8 us; the launch traced here: 39.6 us
  blocking collectives  33.8 us (85%)
  Pallas kernels  5.72 us (14%)
    all_to_all x1, blocking collectives, body(): lax.all_to_all(blocks, ('dom', 'tm'), split_axis=0, concat_axis=0, tiled=...  22.6 us
    all_to_all x1, blocking collectives, body(): lax.all_to_all(incoming, 'dom', split_axis=0, concat_axis=0, tiled=True)  11.2 us
    pallas_call x1, Pallas kernels, body(): pl.pallas_call(aggregate_kernel, out_shape=(jax.ShapeDtypeStruct((N_DOM *...  2.78 us
    pallas_call x1, Pallas kernels, body(): pl.pallas_call(translate_kernel, out_shape=jax.ShapeDtypeStruct((N_DOM, 8...  1.59 us
    pallas_call x1, Pallas kernels, body(): pl.pallas_call(receive_kernel, out_shape=jax.ShapeDtypeStruct((2, PAN_DEV...  1.36 us

profile of v7, /device:TPU:1, one launch (start us, length us, event | category | flops | bytes accessed | tf_op | source)
XLA Modules:
  0.0 39.6 jit_solution(6872593676880665860)
XLA Ops:
  0.0 2.8 %aggregate.1 = (bf16[128,8,128]{2,1,0:T(8,128)(2,1)S(1)}, bf16[512,4096]{1,0:T(8,128)(2,1)S(1)}, f32[256,4096]{1,0:T(8,128)S(1)}, s32[1,1024]{1,0:T(1,128)S(1)}) custom-call(bf16[2,1024]{1,0:T(2,128)(2,1)} %signal_hbm.1, s32[1,1024]{1,0:T(1,128)} %bitcast.12, bf16[1024,1024]{1,0:T(8,128)(2,1)} %radiation_hbm.1, s32[8,512]{1,0:T(8,128)} %bitcast.10, ...), custom_call_target="tpu_custom_call" | custom-call | tf_op jit(solution)/shard_map/aggregate/pallas_call | solution.py:211
  2.8 22.6 %all_to_all.10 = bf16[128,8,128]{2,1,0:T(8,128)(2,1)S(1)} all-to-all(bf16[128,8,128]{2,1,0:T(8,128)(2,1)S(1)} %get-tuple-element.9), channel_id=1, replica_groups=mesh['dom'=32,'tm'=4] {'dom','tm'}, dimensions={0} | all-to-all | bytes 524288 | tf_op jit(solution)/shard_map/all_to_all | solution.py:241
  25.4 0.0 copy-start
  25.4 1.6 %translate.1 = bf16[32,8,128]{2,1,0:T(8,128)(2,1)S(1)} custom-call(bf16[32,4,8,128]{3,2,1,0:T(8,128)(2,1)S(1)} %bitcast.8, bf16[512,4096]{1,0:T(8,128)(2,1)S(1)} %get-tuple-element.10.pick_ref, f32[256,4096]{1,0:T(8,128)S(1)} %get-tuple-element.11.weight_ref), custom_call_target="tpu_custom_call" | custom-call | tf_op jit(solution)/shard_map/translate/pallas_call | solution.py:243
  27.0 11.2 %all_to_all.11.rays_ref = bf16[32,8,128]{2,1,0:T(8,128)(2,1)S(1)} all-to-all(bf16[32,8,128]{2,1,0:T(8,128)(2,1)S(1)} %translate.1), channel_id=1, replica_groups=mesh['dom'=32,'tm'=4] {'dom'}, dimensions={0} | all-to-all | bytes 131072 | tf_op jit(solution)/shard_map/all_to_all | solution.py:257
  38.2 0.0 copy-done
  38.2 1.4 %receive.1 = bf16[2,1024]{1,0:T(2,128)(2,1)} custom-call(bf16[32,8,128]{2,1,0:T(8,128)(2,1)S(1)} %all_to_all.11.rays_ref, s32[1,1024]{1,0:T(1,128)S(1)} %get-tuple-element.12.box_ref, bf16[1024,1024]{1,0:T(8,128)(2,1)S(1)} %copy-done), custom_call_target="tpu_custom_call" | custom-call | tf_op jit(solution)/shard_map/receive/pallas_call | solution.py:258
Async XLA Ops:
  25.4 12.8 %copy-start = (bf16[1024,1024]{1,0:T(8,128)(2,1)S(1)}, bf16[1024,1024]{1,0:T(8,128)(2,1)}, u32[]{:S(2)}) copy-start(bf16[1024,1024]{1,0:T(8,128)(2,1)} %reception_ref.1) | copy-start | bytes 6291460

commit v8 on v7

--- a/solution.py
+++ b/solution.py
@@ -58,7 +58,7 @@
 
     row = lax.broadcasted_iota(jnp.int32, (16, 128), 0)
     pattern = row // 8 * BOX_DEV + row % 8
-    kind = lax.broadcasted_iota(jnp.int32, (CLASSES, 128), 0)
+    kind = lax.broadcasted_iota(jnp.int32, (CLASSES, 128), 0).astype(jnp.int16)
     one, zero = jnp.bfloat16(1), jnp.bfloat16(0)
     for copy in copies[:4]:
         copy.wait()
@@ -87,10 +87,14 @@
             )
     for chunk in range(N_CHUNK):
         lanes = slice(chunk * 128, chunk * 128 + 128)
-        hots = [
-            (classes[j : j + 1, lanes] == kind).astype(jnp.float32).astype(jnp.bfloat16)
-            for j in range(J)
-        ]
+        hots = []
+        for j in range(J):
+            wanted = jnp.broadcast_to(classes[j : j + 1, lanes], (16, 128)).astype(jnp.int16)
+            parts = [
+                jnp.where(wanted == kind[low : low + 16], one, zero)
+                for low in range(0, CLASSES, 16)
+            ]
+            hots.append(jnp.concatenate(parts, axis=0))
         at = slice(chunk * J * 128, (chunk + 1) * J * 128)
         weight_ref[:, at] = jnp.dot(
             lagged, jnp.concatenate(hots, axis=1), preferred_element_type=jnp.float32

time: 39.8 us -> 39.8 us (level)
  no operation moved by 1% of the time
where the time goes in v8:
time: 39.8 us; the launch traced here: 39.6 us
  blocking collectives  33.8 us (85%)
  Pallas kernels  5.72 us (14%)
    all_to_all x1, blocking collectives, body(): lax.all_to_all(blocks, ('dom', 'tm'), split_axis=0, concat_axis=0, tiled=...  22.6 us
    all_to_all x1, blocking collectives, body(): lax.all_to_all(incoming, 'dom', split_axis=0, concat_axis=0, tiled=True)  11.2 us
    pallas_call x1, Pallas kernels, body(): pl.pallas_call(aggregate_kernel, out_shape=(jax.ShapeDtypeStruct((N_DOM *...  2.77 us
    pallas_call x1, Pallas kernels, body(): pl.pallas_call(translate_kernel, out_shape=jax.ShapeDtypeStruct((N_DOM, 8...  1.59 us
    pallas_call x1, Pallas kernels, body(): pl.pallas_call(receive_kernel, out_shape=jax.ShapeDtypeStruct((2, PAN_DEV...  1.36 us

profile of v8, /device:TPU:1, one launch (start us, length us, event | category | flops | bytes accessed | tf_op | source)
XLA Modules:
  0.0 39.6 jit_solution(10630509474907958573)
XLA Ops:
  0.0 2.8 %aggregate.1 = (bf16[128,8,128]{2,1,0:T(8,128)(2,1)S(1)}, bf16[512,4096]{1,0:T(8,128)(2,1)S(1)}, f32[256,4096]{1,0:T(8,128)S(1)}, s32[1,1024]{1,0:T(1,128)S(1)}) custom-call(bf16[2,1024]{1,0:T(2,128)(2,1)} %signal_hbm.1, s32[1,1024]{1,0:T(1,128)} %bitcast.12, bf16[1024,1024]{1,0:T(8,128)(2,1)} %radiation_hbm.1, s32[8,512]{1,0:T(8,128)} %bitcast.10, ...), custom_call_target="tpu_custom_call" | custom-call | tf_op jit(solution)/shard_map/aggregate/pallas_call | solution.py:215
  2.8 22.6 %all_to_all.10 = bf16[128,8,128]{2,1,0:T(8,128)(2,1)S(1)} all-to-all(bf16[128,8,128]{2,1,0:T(8,128)(2,1)S(1)} %get-tuple-element.9), channel_id=1, replica_groups=mesh['dom'=32,'tm'=4] {'dom','tm'}, dimensions={0} | all-to-all | bytes 524288 | tf_op jit(solution)/shard_map/all_to_all | solution.py:245
  25.4 0.0 copy-start
  25.4 1.6 %translate.1 = bf16[32,8,128]{2,1,0:T(8,128)(2,1)S(1)} custom-call(bf16[32,4,8,128]{3,2,1,0:T(8,128)(2,1)S(1)} %bitcast.8, bf16[512,4096]{1,0:T(8,128)(2,1)S(1)} %get-tuple-element.10.pick_ref, f32[256,4096]{1,0:T(8,128)S(1)} %get-tuple-element.11.weight_ref), custom_call_target="tpu_custom_call" | custom-call | tf_op jit(solution)/shard_map/translate/pallas_call | solution.py:247
  27.0 11.2 %all_to_all.11.rays_ref = bf16[32,8,128]{2,1,0:T(8,128)(2,1)S(1)} all-to-all(bf16[32,8,128]{2,1,0:T(8,128)(2,1)S(1)} %translate.1), channel_id=1, replica_groups=mesh['dom'=32,'tm'=4] {'dom'}, dimensions={0} | all-to-all | bytes 131072 | tf_op jit(solution)/shard_map/all_to_all | solution.py:261
  38.2 0.0 copy-done
  38.2 1.4 %receive.1 = bf16[2,1024]{1,0:T(2,128)(2,1)} custom-call(bf16[32,8,128]{2,1,0:T(8,128)(2,1)S(1)} %all_to_all.11.rays_ref, s32[1,1024]{1,0:T(1,128)S(1)} %get-tuple-element.12.box_ref, bf16[1024,1024]{1,0:T(8,128)(2,1)S(1)} %copy-done), custom_call_target="tpu_custom_call" | custom-call | tf_op jit(solution)/shard_map/receive/pallas_call | solution.py:262
Async XLA Ops:
  25.4 12.8 %copy-start = (bf16[1024,1024]{1,0:T(8,128)(2,1)S(1)}, bf16[1024,1024]{1,0:T(8,128)(2,1)}, u32[]{:S(2)}) copy-start(bf16[1024,1024]{1,0:T(8,128)(2,1)} %reception_ref.1) | copy-start | bytes 6291460
